TPU v7x, 512 devices: a whole 4x8x8 slice. The times are simulated.
512 devices in a mesh: row: 32 (over z, y_hi), col: 16 (over y_lo, x, core).
Axes of the slice: x: 4, y: 8 (y_hi: 4, y_lo: 2; y = y_hi * 2 + y_lo), z: 8, core: 2. Of those that a mesh axis runs over, the one named last changes fastest.
Arguments:
- pair: bfloat16 [256, 2048, 128], P('row', 'col'), may hold values from -6 to 6
- panel_left: bfloat16 [256, 2048, 128], P('row', 'col'), may hold values from -6 to 6
- panel_right: bfloat16 [2048, 2048, 128], P('row', 'col'), may hold values from -6 to 6
- single: bfloat16 [2048, 384], P('row'), may hold values from -6 to 6
- token_mask: int32 [2048], P('row'), may hold values from 0 to 1, as said below
- chain_ids: int32 [2048], P('row'), may hold values from 0 to 3, never falling along the last dimension, each value on 1 to 1024 neighbouring positions
- w_tri_gate: bfloat16 [128, 128], replicated, may hold values from -0.5 to 0.5
- w_tri_out: bfloat16 [128, 128], replicated, may hold values from -0.5 to 0.5
- w_trans_in: bfloat16 [128, 1024], replicated, may hold values from -0.5 to 0.5
- w_trans_down: bfloat16 [512, 128], replicated, may hold values from -0.25 to 0.25
- w_bias: bfloat16 [128, 16], replicated, may hold values from -1.5 to 1.5
- chain_bias: float32 [16], replicated, may hold values from -2 to 2
- w_attn: bfloat16 [4, 384, 384], P(None, None, 'col'), may hold values from -0.3125 to 0.3125
- w_attn_out: bfloat16 [384, 384], P('col'), may hold values from -0.3125 to 0.3125
Outputs:
- pair_out: bfloat16 [256, 2048, 128], P('row', 'col')
- single_out: bfloat16 [256, 384], P('row')
Inputs may be any that keep to these rules, and one draw needn't show every extreme that they name: `token_mask`: each entry is 0 or 1; the first token of every aligned block of 64 tokens is 1.
All inputs are finite; a program needn't handle non-finite values.
Results may differ from a plain program's by a relative error of at most 0.0075.
Values may be sent and summed in bfloat16 or wider, within the bound.
A program may use at most 64 MiB of HBM per device.

v0:
```python
import jax
import jax.numpy as jnp
from jax import lax
from jax.sharding import PartitionSpec as P

HEAD_DIM = 24


epsilon = 1e-05


def from_root(value, axis, source):
    kept = jnp.where(lax.axis_index(axis) == source, value, 0).astype(value.dtype)
    return lax.psum(kept, axis)


def layer_norm(values, axis):
    mean_val = jnp.mean(values, axis=axis, keepdims=True)
    centred = values - mean_val
    variance = jnp.mean(centred * centred, axis=axis, keepdims=True)
    return centred * lax.rsqrt(variance + epsilon)


def pair_bias(bias_norm, w_bias, chain_bias, chain_rows, chain_cols):
    linear_part = jnp.einsum("ijc,ch->hij", bias_norm, w_bias, preferred_element_type=jnp.float32)
    same_chain = (chain_rows[:, None] == chain_cols[None, :]).astype(jnp.float32)
    return linear_part + chain_bias[:, None, None] * same_chain[None]


def local(
    pair,
    panel_left,
    panel_right,
    single,
    token_mask,
    chain_ids,
    w_tri_gate,
    w_tri_out,
    w_trans_in,
    w_trans_down,
    w_bias,
    chain_bias,
    w_attn,
    w_attn_out,
):
    rows_own = pair.shape[0]
    cols_own = pair.shape[1]
    col_index = lax.axis_index("col")
    left_first = jnp.transpose(panel_left, (2, 0, 1))
    right_first = jnp.transpose(panel_right, (2, 0, 1))
    left_moved = lax.all_to_all(left_first, "row", split_axis=0, concat_axis=1, tiled=True)
    right_moved = lax.all_to_all(
        lax.all_to_all(right_first, "row", split_axis=0, concat_axis=1, tiled=True),
        "col",
        split_axis=1,
        concat_axis=2,
        tiled=True,
    )
    tri_part = lax.dot_general(
        lax.all_gather(left_moved, "col", axis=2, tiled=True),
        right_moved,
        (((2,), (2,)), ((0,), (0,))),
        preferred_element_type=jnp.float32,
    )
    tri_full = lax.all_to_all(
        tri_part.astype(jnp.bfloat16), "row", split_axis=1, concat_axis=0, tiled=True
    )
    pair_norm = layer_norm(pair.astype(jnp.float32), -1).astype(jnp.bfloat16)
    gate_tri = jax.nn.sigmoid(jnp.dot(pair_norm, w_tri_gate, preferred_element_type=jnp.float32))
    tri_norm = layer_norm(tri_full.astype(jnp.float32), 0).astype(jnp.bfloat16)
    projected = jnp.einsum("cij,cd->ijd", tri_norm, w_tri_out, preferred_element_type=jnp.float32)
    pair_mid = pair.astype(jnp.float32) + gate_tri * projected
    hidden_width = w_trans_down.shape[0]
    trans_in = layer_norm(pair_mid, -1).astype(jnp.bfloat16)
    both_parts = jnp.dot(trans_in, w_trans_in, preferred_element_type=jnp.float32)
    trans_act = (
        jax.nn.silu(both_parts[..., :hidden_width]) * both_parts[..., hidden_width:]
    ).astype(jnp.bfloat16)
    pair_out = (
        pair_mid + jnp.dot(trans_act, w_trans_down, preferred_element_type=jnp.float32)
    ).astype(jnp.bfloat16)
    bias_norm = layer_norm(pair_out.astype(jnp.float32), -1).astype(jnp.bfloat16)
    chain_rows = chain_ids[:rows_own]
    single_norm = layer_norm(single.astype(jnp.float32), -1).astype(jnp.bfloat16)
    query_in = single_norm[:rows_own]
    score_scale = HEAD_DIM ** (-0.5)
    weights_full = lax.all_gather(w_attn, "col", axis=2, tiled=True)
    out_full = lax.all_gather(w_attn_out, "col", axis=0, tiled=True)
    mask_all, chain_all = (
        lax.all_gather(token_mask, "row", axis=0, tiled=True),
        lax.all_gather(chain_ids, "row", axis=0, tiled=True),
    )
    group_size = lax.axis_size("row") // lax.axis_size("col")
    block_parts = []
    for member in range(group_size):
        source_row = col_index * group_size + member
        block_parts.append(from_root(single, "row", source_row))
    key_rows_in = jnp.concatenate(block_parts, axis=0)
    key_norm = layer_norm(key_rows_in.astype(jnp.float32), -1).astype(jnp.bfloat16)
    mask_cols = lax.dynamic_slice_in_dim(mask_all, col_index * cols_own, cols_own, 0).astype(
        jnp.float32
    )
    chain_cols = lax.dynamic_slice_in_dim(chain_all, col_index * cols_own, cols_own, 0)
    bias_tile = pair_bias(bias_norm, w_bias, chain_bias, chain_rows, chain_cols)
    full_width = weights_full.shape[2]
    head_total = full_width // HEAD_DIM
    queries = (
        jnp.dot(query_in, weights_full[0], preferred_element_type=jnp.float32) * score_scale
    ).astype(jnp.bfloat16)
    queries = queries.reshape(rows_own, head_total, HEAD_DIM)
    key_value_weights = jnp.concatenate((weights_full[1], weights_full[2]), axis=1)
    key_value = jnp.dot(key_norm, key_value_weights, preferred_element_type=jnp.float32).astype(
        jnp.bfloat16
    )
    keys_heads = key_value[:, :full_width].reshape(cols_own, head_total, HEAD_DIM)
    values_heads = key_value[:, full_width:].reshape(cols_own, head_total, HEAD_DIM)
    scores = (
        jnp.einsum("ihd,jhd->hij", queries, keys_heads, preferred_element_type=jnp.float32)
        + bias_tile
    )
    weights = jnp.exp(scores) * mask_cols[None, None, :]
    denominator_part = jnp.sum(weights, axis=2)
    numerator_part = jnp.einsum(
        "hij,jhd->ihd",
        weights.astype(jnp.bfloat16),
        values_heads,
        preferred_element_type=jnp.float32,
    )
    numerator, denominator = lax.psum((numerator_part, denominator_part), "col")
    attended = (numerator / jnp.transpose(denominator)[:, :, None]).reshape(rows_own, full_width)
    gate_single = jax.nn.sigmoid(
        jnp.dot(query_in, weights_full[3], preferred_element_type=jnp.float32)
    )
    gated = (gate_single * attended).astype(jnp.bfloat16)
    mixed = jnp.dot(gated, out_full, preferred_element_type=jnp.float32)
    single_out = (single[:rows_own].astype(jnp.float32) + mixed).astype(jnp.bfloat16)
    return (pair_out, single_out)


def solution(mesh):
    in_specs = (
        P("row", "col", None),
        P("row", "col", None),
        P("row", "col", None),
        P("row", None),
        P("row"),
        P("row"),
        P(),
        P(),
        P(),
        P(),
        P(),
        P(),
        P(None, None, "col"),
        P("col", None),
    )
    out_specs = (P("row", "col", None), P("row", None))
    return jax.shard_map(local, mesh=mesh, in_specs=in_specs, out_specs=out_specs, check_vma=False)
```

profile of v0, /device:TPU:1, one launch (start us, length us, event | category | flops | bytes accessed | tf_op | source)
XLA Modules:
  0.0 436.6 jit_solution(6772383447535086083)
XLA Ops:
  8.1 1.5 broadcast_select_fusion.1
  10.1 1.8 copy.52
  12.0 16.5 %all-to-all-start = ((bf16[128,8,128]{2,1,0:T(8,128)(2,1)}), bf16[128,8,128]{2,1,0:T(8,128)(2,1)S(1)}, u32[]{:S(2)}, u32[]{:S(2)}) async-start(bf16[128,8,128]{2,1,0:T(8,128)(2,1)} %bitcast.1), calls=%async_computation | async-start | bytes 524288 | tf_op jit(solution)/shard_map/all_to_all | solution.py:51
  28.5 4.2 copy.54
  32.7 8.2 %all-to-all-done = bf16[128,8,128]{2,1,0:T(8,128)(2,1)S(1)} async-done(((bf16[128,8,128]{2,1,0:T(8,128)(2,1)}), bf16[128,8,128]{2,1,0:T(8,128)(2,1)S(1)}, u32[]{:S(2)}, u32[]{:S(2)}) %all-to-all-start) | async-done | bytes 262176 | tf_op jit(solution)/shard_map/all_to_all | solution.py:51
  40.8 6.2 %all-to-all-start.1 = ((bf16[128,64,128]{2,1,0:T(8,128)(2,1)}), bf16[128,64,128]{2,1,0:T(8,128)(2,1)S(1)}, u32[]{:S(2)}, u32[]{:S(2)}) async-start(bf16[128,64,128]{2,1,0:T(8,128)(2,1)} %bitcast.5), calls=%async_computation.1 | async-start | bytes 4194304 | tf_op jit(solution)/shard_map/all_to_all | solution.py:53
  47.9 63.5 %all-to-all-done.1 = bf16[128,64,128]{2,1,0:T(8,128)(2,1)S(1)} async-done(((bf16[128,64,128]{2,1,0:T(8,128)(2,1)}), bf16[128,64,128]{2,1,0:T(8,128)(2,1)S(1)}, u32[]{:S(2)}, u32[]{:S(2)}) %all-to-all-start.1) | async-done | bytes 2097184 | tf_op jit(solution)/shard_map/all_to_all | solution.py:53
  111.6 10.8 %copy.56 = bf16[4,2048,128]{2,0,1:T(4,128)(2,1)} copy(bf16[4,2048,128]{2,1,0:T(8,128)(2,1)S(1)} %bitcast.79) | data formatting | bytes 4194304 | tf_op jit(solution)/shard_map/all_to_all | solution.py:53
  122.4 5.5 %all-to-all-start.2 = ((bf16[4,2048,128]{2,0,1:T(4,128)(2,1)}), bf16[4,2048,128]{2,0,1:T(4,128)(2,1)S(1)}, u32[]{:S(2)}, u32[]{:S(2)}) async-start(bf16[4,2048,128]{2,0,1:T(4,128)(2,1)} %copy.56), calls=%async_computation.2 | async-start | bytes 4194304 | tf_op jit(solution)/shard_map/all_to_all | solution.py:52
  128.1 1.3 dynamic-slice
  130.6 144.8 %all-reduce.2 = (s32[2048]{0:T(1024)S(1)}, s32[2048]{0:T(1024)S(1)}) all-reduce(s32[2048]{0:T(1024)S(1)} %dynamic-update-slice.1, s32[2048]{0:T(1024)S(1)} %dynamic-update-slice), channel_id=1, replica_groups=mesh['row'=32,'col'=16] {'row'}, use_global_device_ids=true, to_apply=%add.1 | all-reduce | flops 4096 | bytes 32768
  275.8 48.1 %all_gather.19 = bf16[384,384]{1,0:T(8,128)(2,1)S(1)} all-gather(bf16[24,384]{1,0:T(8,128)(2,1)S(1)} %copy-done.9), channel_id=1, replica_groups=mesh['row'=32,'col'=16] {'col'}, dimensions={0}, use_global_device_ids=true | all-gather | bytes 313344 | tf_op jit(solution)/shard_map/all_gather | solution.py:88
  324.9 1.1 fusion.6
  326.0 0.9 convert_reduce_fusion.2
  327.0 1.0 fusion.49
  328.5 1.9 slice_bitcast_fusion.3
  330.4 1.6 copy.57
  332.1 4.1 fusion.9
  336.2 0.9 copy.59
  337.2 5.9 %all-to-all-start.3 = ((bf16[4,256,128]{2,0,1:T(4,128)(2,1)}), bf16[4,256,128]{2,0,1:T(4,128)(2,1)S(1)}, u32[]{:S(2)}, u32[]{:S(2)}) async-start(bf16[4,256,128]{2,0,1:T(4,128)(2,1)} %copy.59), calls=%async_computation.3 | async-start | bytes 524288 | tf_op jit(solution)/shard_map/all_to_all | solution.py:65
  343.6 0.9 fusion.19
  344.8 9.7 %all-to-all-done.3 = bf16[4,256,128]{2,0,1:T(4,128)(2,1)S(1)} async-done(((bf16[4,256,128]{2,0,1:T(4,128)(2,1)}), bf16[4,256,128]{2,0,1:T(4,128)(2,1)S(1)}, u32[]{:S(2)}, u32[]{:S(2)}) %all-to-all-start.3) | async-done | bytes 262176 | tf_op jit(solution)/shard_map/all_to_all | solution.py:65
  358.7 68.6 %all-reduce.3 = (f32[8,16,24]{2,0,1:T(8,128)S(1)}, f32[8,16]{0,1:T(8,128)S(1)}) all-reduce(f32[8,16,24]{2,0,1:T(8,128)S(1)} %convolution_bitcast_fusion, f32[8,16]{0,1:T(8,128)S(1)} %bitcast.88), channel_id=1, replica_groups=mesh['row'=32,'col'=16] {'col'}, use_global_device_ids=true, to_apply=%region_14.15 | all-reduce | flops 3200 | bytes 25600 | tf_op jit(solution)/shard_map/psum | solution.py:129
  427.5 1.7 fusion.20
  (89 shorter events, 9.2 us)
Async XLA Ops:
  8.0 347.4 %copy-start = (bf16[128,1024]{1,0:T(8,128)(2,1)S(1)}, bf16[128,1024]{1,0:T(8,128)(2,1)}, u32[]{:S(2)}) copy-start(bf16[128,1024]{1,0:T(8,128)(2,1)} %param.22) | copy-start | bytes 786436
  8.0 318.0 %all-reduce.7.cloned.1.call-start = ((), (), s32[]{:S(2)}) async-start(), calls=%async_computation.6 | async-start | bytes 196608 | tf_op jit(solution)/shard_map/psum | solution.py:14
  9.6 319.0 %all-gather.5.cloned.1.call-start = ((), (), s32[]{:S(2)}) async-start(), calls=%async_computation.5 | async-start | bytes 1253376 | tf_op jit(solution)/shard_map/all_gather | solution.py:87
  12.0 28.9 %all-to-all-start = ((bf16[128,8,128]{2,1,0:T(8,128)(2,1)}), bf16[128,8,128]{2,1,0:T(8,128)(2,1)S(1)}, u32[]{:S(2)}, u32[]{:S(2)}) async-start(bf16[128,8,128]{2,1,0:T(8,128)(2,1)} %bitcast.1), calls=%async_computation | async-start | bytes 524288 | tf_op jit(solution)/shard_map/all_to_all | solution.py:51
  40.8 70.6 %all-to-all-start.1 = ((bf16[128,64,128]{2,1,0:T(8,128)(2,1)}), bf16[128,64,128]{2,1,0:T(8,128)(2,1)S(1)}, u32[]{:S(2)}, u32[]{:S(2)}) async-start(bf16[128,64,128]{2,1,0:T(8,128)(2,1)} %bitcast.5), calls=%async_computation.1 | async-start | bytes 4194304 | tf_op jit(solution)/shard_map/all_to_all | solution.py:53
  47.1 285.0 %all-gather.3.cloned.1.call-start = ((), (), s32[]{:S(2)}) async-start(), calls=%async_computation.4 | async-start | bytes 4456448 | tf_op jit(solution)/shard_map/all_gather | solution.py:60
  122.4 5.5 %copy-start.5 = (bf16[8,128,128]{2,1,0:T(8,128)(2,1)S(1)}, bf16[8,128,128]{2,1,0:T(8,128)(2,1)}, u32[]{:S(2)}) copy-start(bf16[8,128,128]{2,1,0:T(8,128)(2,1)} %param.14) | copy-start | bytes 786436
  122.4 7.6 %copy-start.11 = (s32[64]{0:T(128)S(1)}, s32[64]{0:T(128)}, u32[]{:S(2)}) copy-start(s32[64]{0:T(128)} %param.19) | copy-start | bytes 772
  122.4 7.9 %copy-start.14 = (s32[64]{0:T(128)S(1)}, s32[64]{0:T(128)}, u32[]{:S(2)}) copy-start(s32[64]{0:T(128)} %param.18) | copy-start | bytes 772
  122.4 153.2 %copy-start.2 = (bf16[64,384]{1,0:T(8,128)(2,1)S(1)}, bf16[64,384]{1,0:T(8,128)(2,1)}, u32[]{:S(2)}) copy-start(bf16[64,384]{1,0:T(8,128)(2,1)} %param.17) | copy-start | bytes 147460
  122.4 153.4 %copy-start.9 = (bf16[24,384]{1,0:T(8,128)(2,1)S(1)}, bf16[24,384]{1,0:T(8,128)(2,1)}, u32[]{:S(2)}) copy-start(bf16[24,384]{1,0:T(8,128)(2,1)} %param.27) | copy-start | bytes 55300
  122.4 208.0 %all-to-all-start.2 = ((bf16[4,2048,128]{2,0,1:T(4,128)(2,1)}), bf16[4,2048,128]{2,0,1:T(4,128)(2,1)S(1)}, u32[]{:S(2)}, u32[]{:S(2)}) async-start(bf16[4,2048,128]{2,0,1:T(4,128)(2,1)} %copy.56), calls=%async_computation.2 | async-start | bytes 4194304 | tf_op jit(solution)/shard_map/all_to_all | solution.py:52
  332.1 11.0 %copy-start.3 = (bf16[384,384]{0,1:T(8,128)(2,1)S(1)}, bf16[384,384]{0,1:T(8,128)(2,1)}, u32[]{:S(2)}) copy-start(bf16[384,384]{0,1:T(8,128)(2,1)} %get-tuple-element.14) | copy-start | bytes 884740
  332.1 11.0 %copy-start.4 = (bf16[384,384]{0,1:T(8,128)(2,1)S(1)}, bf16[384,384]{0,1:T(8,128)(2,1)}, u32[]{:S(2)}) copy-start(bf16[384,384]{0,1:T(8,128)(2,1)} %get-tuple-element.15) | copy-start | bytes 884740
  332.1 11.0 %copy-start.6 = (bf16[64,384]{1,0:T(8,128)(2,1)S(1)}, bf16[64,384]{1,0:T(8,128)(2,1)}, u32[]{:S(2)}) copy-start(bf16[64,384]{1,0:T(8,128)(2,1)} %get-tuple-element.12) | copy-start | bytes 147460
  332.1 11.0 %copy-start.7 = (bf16[64,384]{1,0:T(8,128)(2,1)S(1)}, bf16[64,384]{1,0:T(8,128)(2,1)}, u32[]{:S(2)}) copy-start(bf16[64,384]{1,0:T(8,128)(2,1)} %get-tuple-element.13) | copy-start | bytes 147460
  332.1 11.0 %copy-start.15 = (f32[128]{0:T(128)S(1)}, f32[128]{0:T(128)}, u32[]{:S(2)}) copy-start(f32[128]{0:T(128)} %add_rsqrt_fusion.4) | copy-start | bytes 1540
  336.2 7.4 %copy-start.1 = (bf16[4,384,384]{1,2,0:T(8,128)(2,1)S(1)}, bf16[4,384,384]{1,2,0:T(8,128)(2,1)}, u32[]{:S(2)}) copy-start(bf16[4,384,384]{1,2,0:T(8,128)(2,1)} %all-gather.5.cloned.1.call-done) | copy-start | bytes 3538948
  337.2 17.3 %all-to-all-start.3 = ((bf16[4,256,128]{2,0,1:T(4,128)(2,1)}), bf16[4,256,128]{2,0,1:T(4,128)(2,1)S(1)}, u32[]{:S(2)}, u32[]{:S(2)}) async-start(bf16[4,256,128]{2,0,1:T(4,128)(2,1)} %copy.59), calls=%async_computation.3 | async-start | bytes 524288 | tf_op jit(solution)/shard_map/all_to_all | solution.py:65
  343.4 11.6 %copy-start.8 = (bf16[128,128]{1,0:T(8,128)(2,1)S(1)}, bf16[128,128]{1,0:T(8,128)(2,1)}, u32[]{:S(2)}) copy-start(bf16[128,128]{1,0:T(8,128)(2,1)} %param.21) | copy-start | bytes 98308
  355.4 0.9 copy-start.12
  356.3 1.8 copy-start.13
  356.3 1.9 copy-start.10
Sparse Core Ops, SparseCore 0:
  11.8 310.2 all-reduce.6
Sparse Core Ops, SparseCore 1:
  12.1 50.0 all-gather.4
  64.7 62.5 all-gather.2
where the time goes:
time: 440 us; the launch traced here: 437 us
  blocking collectives  262 us (60%)
  waiting for transfers between devices  82 us (19%)
  starting transfers between devices  34.2 us (8%)
  local copies, waits for them, and re-layouts  25.9 us (6%)
  between operations  16.6 us (4%)
  matrix products  10.5 us (2%)
  other arithmetic  5.78 us (1%)
    unnamed x1, blocking collectives  145 us
    psum x1, blocking collectives, local(): numerator, denominator = lax.psum((numerator_part, denominator_part), 'col')  68.6 us
    all_to_all x1, waiting for transfers between devices, local(): lax.all_to_all(right_first, 'row', split_axis=0, concat_axis=1, tiled=True)  63.5 us
    all_gather x1, blocking collectives, local(): out_full = lax.all_gather(w_attn_out, 'col', axis=0, tiled=True)  48.1 us
    all_to_all x1, starting transfers between devices, local(): lax.all_to_all(left_first, 'row', split_axis=0, concat_axis=1, tiled=True)  16.5 us
    all_to_all x2, local copies, waits for them, and re-layouts, local(): lax.all_to_all(right_first, 'row', split_axis=0, concat_axis=1, tiled=True)  10.9 us
    all_to_all x1, waiting for transfers between devices, local(): lax.all_to_all(tri_part.astype(jnp.bfloat16), 'row', split_axis=1, concat...  9.72 us
    unnamed x41, local copies, waits for them, and re-layouts  9.08 us
  transfers between devices with their start and end apart: 7, of which 3 were waited for; matrix products, arithmetic and copies ran while one was open for 7% of the time, Pallas kernels for 0%

commit v1 on v0

v1 whole, which is shorter than its diff:
```python
import jax
import jax.numpy as jnp
from jax import lax
from jax.experimental import pallas as pl
from jax.experimental.pallas import tpu as pltpu
from jax.sharding import PartitionSpec as P

HEAD_DIM = 24
HEADS = 16
NZ = 8
NY = 4
NQ = 16
GROUP = NY * NQ
MESH = pl.DeviceIdType.MESH

epsilon = 1e-05


def layer_norm(values, axis):
    mean_val = jnp.mean(values, axis=axis, keepdims=True)
    centred = values - mean_val
    variance = jnp.mean(centred * centred, axis=axis, keepdims=True)
    return centred * lax.rsqrt(variance + epsilon)


def remote(src, dst, send, recv, row, col):
    return pltpu.make_async_remote_copy(
        src_ref=src, dst_ref=dst, send_sem=send, recv_sem=recv, device_id=(row, col), device_id_type=MESH
    )


def exchange_kernel(
    lt, rt, kv, qg, wo, t_out, kv_all, qg_all, wo_all, lbuf, rbuf, tsend,
    own_sem, l_send, l_recv, r_send, r_recv, z_send, z_recv, k_send, k_recv, q_send, q_recv, w_send, w_recv, t_send, t_recv,
):
    row = lax.axis_index("row")
    col = lax.axis_index("col")
    z = row // NY
    yh = row % NY
    me = yh * NQ + col

    def group_device(m):
        return z * NY + m // NQ, m % NQ

    def others(body):
        def step(n, carry):
            body((me + n) % GROUP)
            return carry

        lax.fori_loop(1, GROUP, step, 0)

    def l_block(m):
        source_row, source_col = group_device(m)
        return lbuf.at[pl.ds(source_row * 16, 16), pl.ds(source_col * 128, 128)]

    def r_block(m):
        return rbuf.at[:, pl.ds((m // NQ) * 64, 64), pl.ds((m % NQ) * 128, 128)]

    def l_copy(m, slot):
        return remote(lt.at[m], l_block(slot), l_send.at[m], l_recv.at[slot], *group_device(m))

    def r_copy(m, slot):
        return remote(rt.at[pl.ds(m * 2, 2)], r_block(slot), r_send.at[m], r_recv.at[slot], *group_device(m))

    l_own = pltpu.make_async_copy(lt.at[me], l_block(me), own_sem.at[0])
    l_own.start()
    others(lambda m: l_copy(m, me).start())

    home = row // 2
    k_slot = (row % 2) * NQ + col
    k_own = pltpu.make_async_copy(kv, kv_all.at[k_slot], own_sem.at[1])

    def k_copy(target, slot):
        return remote(kv, kv_all.at[slot], k_send.at[target], k_recv.at[slot], target, home)

    def k_start(n, carry):
        target = (row + n) % (NZ * NY)
        stays = (n == 0) & (home == col)

        @pl.when(stays)
        def _():
            k_own.start()

        @pl.when(jnp.logical_not(stays))
        def _():
            k_copy(target, k_slot).start()

        return carry

    lax.fori_loop(0, NZ * NY, k_start, 0)

    q_own = pltpu.make_async_copy(qg, qg_all.at[col], own_sem.at[2])
    w_own = pltpu.make_async_copy(wo, wo_all.at[col], own_sem.at[3])
    q_own.start()
    w_own.start()

    def q_copy(target, slot):
        return remote(qg, qg_all.at[slot], q_send.at[target], q_recv.at[slot], row, target)

    def w_copy(target, slot):
        return remote(wo, wo_all.at[slot], w_send.at[target], w_recv.at[slot], row, target)

    def q_start(n, carry):
        target = (col + n) % NQ
        q_copy(target, col).start()
        w_copy(target, col).start()
        return carry

    lax.fori_loop(1, NQ, q_start, 0)

    r_own = pltpu.make_async_copy(rt.at[pl.ds(me * 2, 2)], r_block(me), own_sem.at[4])
    r_own.start()
    others(lambda m: r_copy(m, me).start())

    l_own.wait()
    others(lambda m: l_copy(m, m).wait_recv())

    def z_block(plane):
        return lbuf.at[pl.ds(plane * 64, 64), :]

    def z_copy(plane, way, target_z):
        return remote(z_block(plane), z_block(plane), z_send.at[way, plane], z_recv.at[plane], target_z * NY + yh, col)

    up = (z + 1) % NZ
    down = (z + NZ - 1) % NZ
    for step in range(4):
        if step:
            z_copy((z + NZ - step) % NZ, 0, up).wait_recv()
        z_copy((z + NZ - step) % NZ, 0, up).start()
        if step < 3:
            if step:
                z_copy((z + step) % NZ, 1, down).wait_recv()
            z_copy((z + step) % NZ, 1, down).start()
    z_copy((z + 4) % NZ, 0, up).wait_recv()
    z_copy((z + 3) % NZ, 1, down).wait_recv()

    r_own.wait()
    others(lambda m: r_copy(m, m).wait_recv())

    def multiply(tile, carry):
        start = pl.multiple_of(tile * 128, 128)
        rows = lbuf[pl.ds(start, 128), :]
        dims = (((1,), (1,)), ((), ()))
        first = lax.dot_general(rows, rbuf[0], dims, preferred_element_type=jnp.float32)
        second = lax.dot_general(rows, rbuf[1], dims, preferred_element_type=jnp.float32)
        channel = (lax.broadcasted_iota(jnp.int32, first.shape, 0) // 8) % 2
        both = jnp.where(channel == 0, first, second).astype(jnp.bfloat16)
        for half in range(2):
            tsend[half, pl.ds(tile * 8, 8)] = both[:, half * 128 : half * 128 + 128].reshape(8, 16, 128)
        return carry

    lax.fori_loop(0, 4, multiply, 0)

    t_own = pltpu.make_async_copy(tsend.at[col % 2, row], t_out.at[me], own_sem.at[5])

    def t_copy(m, slot):
        return remote(tsend.at[m % 2, m // 2], t_out.at[slot], t_send.at[m], t_recv.at[slot], m // 2, 2 * z + m % 2)

    def t_stays(m):
        return (m // 2 == row) & (2 * z + m % 2 == col)

    def t_start(n, carry):
        m = (me + n) % GROUP
        stays = t_stays(m)

        @pl.when(stays)
        def _():
            t_own.start()

        @pl.when(jnp.logical_not(stays))
        def _():
            t_copy(m, me).start()

        return carry

    lax.fori_loop(0, GROUP, t_start, 0)

    others(lambda m: l_copy(m, me).wait_send())
    others(lambda m: r_copy(m, me).wait_send())
    for step in range(4):
        z_copy((z + NZ - step) % NZ, 0, up).wait_send()
        if step < 3:
            z_copy((z + step) % NZ, 1, down).wait_send()

    def k_wait(n, carry):
        target = (row + n) % (NZ * NY)
        stays = (n == 0) & (home == col)

        @pl.when(jnp.logical_not(stays))
        def _():
            k_copy(target, k_slot).wait_send()

        from_self = (2 * col + n // NQ == row) & (n % NQ == col)

        @pl.when(from_self)
        def _():
            k_own.wait()

        @pl.when(jnp.logical_not(from_self))
        def _():
            k_copy(n, n).wait_recv()

        return carry

    lax.fori_loop(0, NZ * NY, k_wait, 0)
    q_own.wait()
    w_own.wait()

    def q_wait(n, carry):
        target = (col + n) % NQ
        q_copy(target, col).wait_send()
        w_copy(target, col).wait_send()
        q_copy(target, target).wait_recv()
        w_copy(target, target).wait_recv()
        return carry

    lax.fori_loop(1, NQ, q_wait, 0)

    def t_wait(s, carry):
        from_self = (col // 2 == z) & (s == me)

        @pl.when(from_self)
        def _():
            t_own.wait()

        @pl.when(jnp.logical_not(from_self))
        def _():
            t_copy(s, s).wait_recv()

        @pl.when(jnp.logical_not(t_stays(s)))
        def _():
            t_copy(s, me).wait_send()

        return carry

    lax.fori_loop(0, GROUP, t_wait, 0)


def exchange(lt, rt, kv, qg, wo):
    dma = pltpu.SemaphoreType.DMA
    return pl.pallas_call(
        exchange_kernel,
        out_shape=(
            jax.ShapeDtypeStruct((GROUP, 16, 128), jnp.bfloat16),
            jax.ShapeDtypeStruct((2 * NQ, 32, 128), jnp.bfloat16),
            jax.ShapeDtypeStruct((NQ, 8, 128), jnp.float32),
            jax.ShapeDtypeStruct((NQ, 24, 384), jnp.float32),
        ),
        in_specs=[pl.BlockSpec(memory_space=pl.ANY)] * 5,
        out_specs=(pl.BlockSpec(memory_space=pl.ANY),) * 4,
        scratch_shapes=[
            pltpu.VMEM((512, 2048), jnp.bfloat16),
            pltpu.VMEM((2, 256, 2048), jnp.bfloat16),
            pltpu.VMEM((2, 32, 16, 128), jnp.bfloat16),
            dma((6,)),
            dma((GROUP,)),
            dma((GROUP,)),
            dma((GROUP,)),
            dma((GROUP,)),
            dma((2, NZ)),
            dma((NZ,)),
            dma((2 * NQ,)),
            dma((2 * NQ,)),
            dma((NQ,)),
            dma((NQ,)),
            dma((NQ,)),
            dma((NQ,)),
            dma((GROUP,)),
            dma((GROUP,)),
        ],
        compiler_params=pltpu.CompilerParams(has_side_effects=True, vmem_limit_bytes=32 * 1024 * 1024),
        name="exchange",
    )(lt, rt, kv, qg, wo)


def finish_kernel(part, gate, wo, single, out, slots, own_sem, send, recv):
    row = lax.axis_index("row")
    col = lax.axis_index("col")

    def copy(target, slot):
        return remote(part, slots.at[slot], send.at[target], recv.at[slot], row, target)

    own = pltpu.make_async_copy(part, slots.at[col], own_sem)
    own.start()

    def start(n, carry):
        copy((col + n) % NQ, col).start()
        return carry

    lax.fori_loop(1, NQ, start, 0)
    own.wait()

    def wait(n, carry):
        target = (col + n) % NQ
        copy(target, target).wait_recv()
        copy(target, col).wait_send()
        return carry

    lax.fori_loop(1, NQ, wait, 0)
    total = slots[0]
    for n in range(1, NQ):
        total = total + slots[n]
    attended = total[:8] / total[8:]
    gated = (gate[...] * attended).astype(jnp.bfloat16)
    mixed = jnp.dot(gated, wo[...].astype(jnp.bfloat16), preferred_element_type=jnp.float32)
    out[...] = (single[...].astype(jnp.float32) + mixed).astype(jnp.bfloat16)


def finish(part, gate, wo, single):
    dma = pltpu.SemaphoreType.DMA
    return pl.pallas_call(
        finish_kernel,
        out_shape=jax.ShapeDtypeStruct((8, 384), jnp.bfloat16),
        in_specs=[pl.BlockSpec(memory_space=pltpu.VMEM)] * 4,
        out_specs=pl.BlockSpec(memory_space=pltpu.VMEM),
        scratch_shapes=[pltpu.VMEM((NQ, 16, 384), jnp.float32), dma, dma((NQ,)), dma((NQ,))],
        compiler_params=pltpu.CompilerParams(has_side_effects=True, vmem_limit_bytes=16 * 1024 * 1024),
        name="finish",
    )(part, gate, wo, single)


def local(
    pair,
    panel_left,
    panel_right,
    single,
    token_mask,
    chain_ids,
    w_tri_gate,
    w_tri_out,
    w_trans_in,
    w_trans_down,
    w_bias,
    chain_bias,
    w_attn,
    w_attn_out,
):
    rows_own = pair.shape[0]
    cols_own = pair.shape[1]
    lt = jnp.transpose(panel_left, (2, 0, 1)).reshape(GROUP, 16, 128)
    rt = jnp.transpose(panel_right, (2, 0, 1))

    single_norm = layer_norm(single.astype(jnp.float32), -1).astype(jnp.bfloat16)
    query_in = single_norm[:rows_own]
    score_scale = HEAD_DIM ** (-0.5)
    kv_own = jnp.dot(
        single_norm, jnp.concatenate((w_attn[1], w_attn[2]), axis=1), preferred_element_type=jnp.float32
    ).astype(jnp.bfloat16)
    marks = jnp.stack((token_mask, chain_ids), axis=1).astype(jnp.bfloat16)
    kv = jnp.concatenate(
        (kv_own[:32], kv_own[32:], marks[:32], marks[32:], jnp.zeros((32, 28), jnp.bfloat16)), axis=1
    )
    query_own = (jnp.dot(query_in, w_attn[0], preferred_element_type=jnp.float32) * score_scale).astype(jnp.bfloat16)
    gate_own = jax.nn.sigmoid(jnp.dot(query_in, w_attn[3], preferred_element_type=jnp.float32))
    qg = jnp.concatenate((query_own.astype(jnp.float32), gate_own, jnp.zeros((8, 80), jnp.float32)), axis=1)

    t_out, kv_all, qg_all, wo_all = exchange(lt, rt, kv, qg, w_attn_out.astype(jnp.float32))

    tri_full = t_out.reshape(128, rows_own, cols_own)
    pair_norm = layer_norm(pair.astype(jnp.float32), -1).astype(jnp.bfloat16)
    gate_tri = jax.nn.sigmoid(jnp.dot(pair_norm, w_tri_gate, preferred_element_type=jnp.float32))
    tri_norm = layer_norm(tri_full.astype(jnp.float32), 0).astype(jnp.bfloat16)
    projected = jnp.einsum("cij,cd->ijd", tri_norm, w_tri_out, preferred_element_type=jnp.float32)
    pair_mid = pair.astype(jnp.float32) + gate_tri * projected
    hidden_width = w_trans_down.shape[0]
    trans_in = layer_norm(pair_mid, -1).astype(jnp.bfloat16)
    both_parts = jnp.dot(trans_in, w_trans_in, preferred_element_type=jnp.float32)
    trans_act = (
        jax.nn.silu(both_parts[..., :hidden_width]) * both_parts[..., hidden_width:]
    ).astype(jnp.bfloat16)
    pair_out = (
        pair_mid + jnp.dot(trans_act, w_trans_down, preferred_element_type=jnp.float32)
    ).astype(jnp.bfloat16)
    bias_norm = layer_norm(pair_out.astype(jnp.float32), -1).astype(jnp.bfloat16)

    by_head = kv_all.reshape(2, HEADS, 32, 128)
    halves = jnp.stack((by_head[..., :48], by_head[..., 48:96]), axis=2)
    tokens = jnp.transpose(halves, (1, 0, 2, 3, 4)).reshape(HEADS, cols_own, 48)
    keys_heads = tokens[..., :HEAD_DIM]
    values_heads = tokens[..., HEAD_DIM:]
    marks_all = by_head[:, 0, :, 96:100].astype(jnp.float32)
    mask_cols = jnp.stack((marks_all[..., 0], marks_all[..., 2]), axis=1).reshape(cols_own)
    chain_cols = jnp.stack((marks_all[..., 1], marks_all[..., 3]), axis=1).reshape(cols_own)
    chain_rows = chain_ids[:rows_own].astype(jnp.float32)

    linear_part = jnp.einsum("ijc,ch->hij", bias_norm, w_bias, preferred_element_type=jnp.float32)
    same_chain = (chain_rows[:, None] == chain_cols[None, :]).astype(jnp.float32)
    bias_tile = linear_part + chain_bias[:, None, None] * same_chain[None]
    queries = qg_all[..., :HEAD_DIM].astype(jnp.bfloat16)
    gate = jnp.transpose(qg_all[..., HEAD_DIM : 2 * HEAD_DIM], (1, 0, 2)).reshape(rows_own, HEADS * HEAD_DIM)
    scores = (
        jnp.einsum("hid,hjd->hij", queries, keys_heads, preferred_element_type=jnp.float32) + bias_tile
    )
    weights = jnp.exp(scores) * mask_cols[None, None, :]
    denominator = jnp.sum(weights, axis=2)
    numerator = jnp.einsum(
        "hij,hjd->ihd", weights.astype(jnp.bfloat16), values_heads, preferred_element_type=jnp.float32
    ).reshape(rows_own, HEADS * HEAD_DIM)
    denominator = jnp.repeat(jnp.transpose(denominator), HEAD_DIM, axis=1)
    part = jnp.concatenate((numerator, denominator), axis=0)
    single_out = finish(part, gate, wo_all.reshape(HEADS * HEAD_DIM, 384), single[:rows_own])
    return (pair_out, single_out)


def solution(mesh):
    in_specs = (
        P("row", "col", None),
        P("row", "col", None),
        P("row", "col", None),
        P("row", None),
        P("row"),
        P("row"),
        P(),
        P(),
        P(),
        P(),
        P(),
        P(),
        P(None, None, "col"),
        P("col", None),
    )
    out_specs = (P("row", "col", None), P("row", None))
    return jax.shard_map(local, mesh=mesh, in_specs=in_specs, out_specs=out_specs, check_vma=False)
```

time: 440 us -> 151 us (0.34)
  blocking collectives: 262 us -> 0 us
  Pallas kernels: 0 us -> 131 us
  waiting for transfers between devices: 82 us -> 0 us
  starting transfers between devices: 34.2 us -> 0 us
  local copies, waits for them, and re-layouts: 25.9 us -> 9.28 us
  between operations: 16.6 us -> 1.03 us
  matrix products: 10.5 us -> 4.96 us
    unnamed x1 -> x0, blocking collectives: 145 us -> none
    pallas_call x0 -> x2, Pallas kernels: none -> 131 us  [the longest x1 108 us: exchange(): pl.pallas_call(exchange_kernel, out_shape=(jax.ShapeDtypeStruct((GROUP, 1...]
    all_to_all x4 -> x0, waiting for transfers between devices: 81.4 us -> none  [the longest x1 63.5 us: local(): lax.all_to_all(right_first, 'row', split_axis=0, concat_axis=1, tiled=True)]
    psum x1 -> x0, blocking collectives: 68.6 us -> none  [local(): numerator, denominator = lax.psum((numerator_part, denominator_part), 'col')]
    all_gather x1 -> x0, blocking collectives: 48.1 us -> none  [local(): out_full = lax.all_gather(w_attn_out, 'col', axis=0, tiled=True)]
    all_to_all x4 -> x0, starting transfers between devices: 34.1 us -> none  [the longest x1 16.5 us: local(): lax.all_to_all(left_first, 'row', split_axis=0, concat_axis=1, tiled=True)]
    all_to_all x4 -> x0, local copies, waits for them, and re-layouts: 13.3 us -> none  [the longest x2 10.9 us: local(): lax.all_to_all(right_first, 'row', split_axis=0, concat_axis=1, tiled=True)]
    dot_general x7 -> x6, matrix products: 7.63 us -> 2.81 us  [the longest x1 0.85 us: local(): jnp.dot(query_in, w_attn[0], preferred_element_type=jnp.float32)]
  transfers between devices with their start and end apart: 7 -> 0, of which waited for: 3 -> 0; matrix products, arithmetic and copies ran while one was open for 7% -> 0% of each run, Pallas kernels for 0% -> 0%
where the time goes in v1:
time: 151 us
  Pallas kernels  131 us (87%)
  local copies, waits for them, and re-layouts  9.28 us (6%)
  matrix products  4.96 us (3%)
  other arithmetic  4.37 us (3%)
    pallas_call x1, Pallas kernels, exchange(): pl.pallas_call(exchange_kernel, out_shape=(jax.ShapeDtypeStruct((GROUP, 1...  108 us
    pallas_call x1, Pallas kernels, finish(): pl.pallas_call(finish_kernel, out_shape=jax.ShapeDtypeStruct((8, 384), jn...  22.9 us
    unnamed x25, local copies, waits for them, and re-layouts  6.24 us

profile of v1, /device:TPU:1, one launch (start us, length us, event | category | flops | bytes accessed | tf_op | source)
XLA Modules:
  0.0 150.8 jit_solution(1386706063714463370)
XLA Ops:
  0.6 0.9 convert_reduce_fusion.3
  1.6 1.0 fusion.40
  2.6 0.9 fusion.41
  3.5 0.7 slice_bitcast_fusion.2
  4.4 0.7 convert_bitcast_fusion
  5.5 0.8 fusion.10
  6.3 0.9 fusion.12
  7.3 3.3 %copy.65 = bf16[64,128,128]{1,0,2:T(8,128)(2,1)S(1)} copy(bf16[64,128,128]{2,1,0:T(8,128)(2,1)} %param.16) | data formatting | bytes 4194304 | tf_op args[2]
  10.7 0.2 copy.64
  10.9 108.2 %exchange.1 = (bf16[64,16,128]{2,1,0:T(8,128)(2,1)S(1)}, bf16[32,32,128]{2,1,0:T(8,128)(2,1)S(1)}, f32[16,8,128]{2,1,0:T(8,128)S(1)}, f32[16,24,384]{2,1,0:T(8,128)S(1)}) custom-call(bf16[64,16,128]{2,1,0:T(8,128)(2,1)S(1)} %bitcast.76, bf16[128,64,128]{2,1,0:T(8,128)(2,1)S(1)} %bitcast.71, bf16[32,128]{1,0:T(8,128)(2,1)S(1)} %concatenate.13.kv, ...), custom_call_target="tpu_custom_call" | custom-call | tf_op jit(solution)/shard_map/exchange/pallas_call | solution.py:241
  119.4 1.1 copy.61
  120.7 0.3 fusion.3
  121.1 0.3 fusion.60
  121.5 0.7 fusion.24
  122.2 0.2 copy-done.6
  122.4 0.8 convert_reduce_fusion.1
  123.3 0.2 fusion.25
  124.0 0.1 fusion.57
  124.3 0.5 fusion.61
  124.8 0.3 convolution_bitcast_fusion
  125.7 0.7 slice.96.single
  126.4 22.9 %finish.1 = bf16[8,384]{1,0:T(8,128)(2,1)S(1)} custom-call(f32[16,384]{1,0:T(8,128)S(1)} %pad_maximum_fusion.1.part, f32[8,384]{1,0:T(8,128)S(1)} %reshape.128.gate, f32[384,384]{1,0:T(8,128)S(1)} %bitcast.77, bf16[8,384]{1,0:T(8,128)(2,1)S(1)} %slice.96.single), custom_call_target="tpu_custom_call" | custom-call | tf_op jit(solution)/shard_map/finish/pallas_call | solution.py:311
  149.3 0.9 copy.85
  150.2 0.6 copy.115
  (70 shorter events, 2.5 us)
Async XLA Ops:
  0.6 120.8 %copy-start = (bf16[128,1024]{1,0:T(8,128)(2,1)S(1)}, bf16[128,1024]{1,0:T(8,128)(2,1)}, u32[]{:S(2)}) copy-start(bf16[128,1024]{1,0:T(8,128)(2,1)} %param.22) | copy-start | bytes 786436
  7.3 3.4 %copy-start.1 = (bf16[8,128,128]{2,1,0:T(8,128)(2,1)S(1)}, bf16[8,128,128]{2,1,0:T(8,128)(2,1)}, u32[]{:S(2)}) copy-start(bf16[8,128,128]{2,1,0:T(8,128)(2,1)} %param.15) | copy-start | bytes 786436
  7.3 3.6 %copy-start.3 = (bf16[24,384]{1,0:T(8,128)(2,1)S(1)}, bf16[24,384]{1,0:T(8,128)(2,1)}, u32[]{:S(2)}) copy-start(bf16[24,384]{1,0:T(8,128)(2,1)} %param.27) | copy-start | bytes 55300
  119.1 1.6 %copy-start.7 = (bf16[128,128]{1,0:T(8,128)(2,1)S(1)}, bf16[128,128]{1,0:T(8,128)(2,1)}, u32[]{:S(2)}) copy-start(bf16[128,128]{1,0:T(8,128)(2,1)} %param.20) | copy-start | bytes 98308
  119.3 1.8 %copy-start.2 = (bf16[128,128]{1,0:T(8,128)(2,1)S(1)}, bf16[128,128]{1,0:T(8,128)(2,1)}, u32[]{:S(2)}) copy-start(bf16[128,128]{1,0:T(8,128)(2,1)} %param.21) | copy-start | bytes 98308
  121.5 0.9 copy-start.6
  122.4 0.9 copy-start.8
  122.4 1.4 copy-start.4
  123.2 1.1 copy-start.5

commit v2 on v0

v2 whole, which is shorter than its diff:
```python
import jax
import jax.numpy as jnp
from jax import lax
from jax.experimental import pallas as pl
from jax.experimental.pallas import tpu as pltpu
from jax.sharding import PartitionSpec as P

HEAD_DIM = 24
HEADS = 16
NZ = 8
NY = 4
NQ = 16
GROUP = NY * NQ
SLOT = 32
WIDE = HEADS * SLOT
MESH = pl.DeviceIdType.MESH
EARLY = 24

epsilon = 1e-05


def layer_norm(values, axis):
    mean_val = jnp.mean(values, axis=axis, keepdims=True)
    centred = values - mean_val
    variance = jnp.mean(centred * centred, axis=axis, keepdims=True)
    return centred * lax.rsqrt(variance + epsilon)


def remote(src, dst, send, recv, row, col):
    return pltpu.make_async_remote_copy(
        src_ref=src, dst_ref=dst, send_sem=send, recv_sem=recv, device_id=(row, col), device_id_type=MESH
    )


def dot(a, b, over_a, over_b):
    return lax.dot_general(a, b, (((over_a,), (over_b,)), ((), ())), preferred_element_type=jnp.float32)


def block_kernel(
    lt, rt, pair, single, w_gate, w_out, w_in, w_down, mask_any, chain_any, bias_any, w_bias_any, w_attn_any, w_attn_out_any,
    pair_out, single_out,
    lbuf, rbuf, tsend, tin, tin32, gate_tri, kv_msg, kv_all, qg_msg, qg_all, wo_msg, wo_all, proj_in, square,
    q_full, gate_full, bias_all, part, parts, mask_in, chain_in, chain_bias, bias_weights, w_attn, w_attn_out,
    values_low, own_values_kept, own_sum_kept, mask_kept,
    own_sem, in_sem, l_send, l_recv, r_send, r_recv, z_send, z_recv, k_send, k_recv, kz_send, kz_recv,
    q_send, q_recv, w_send, w_recv, t_send, t_recv, p_send, p_recv,
):
    row = lax.axis_index("row")
    col = lax.axis_index("col")
    z = row // NY
    yh = row % NY
    me = yh * NQ + col
    up = lax.rem(z + 1, NZ)
    down = lax.rem(z + NZ - 1, NZ)

    def group_device(m):
        return z * NY + lax.div(m, NQ), lax.rem(m, NQ)

    def others(body, start=1, stop=GROUP):
        def step(n, carry):
            body(lax.rem(me + n, GROUP))
            return carry

        lax.fori_loop(start, stop, step, 0)

    barrier = pltpu.get_barrier_semaphore()

    def greet(m):
        pl.semaphore_signal(barrier, inc=1, device_id=group_device(m), device_id_type=MESH)

    for plane in (up, down):
        pl.semaphore_signal(barrier, inc=1, device_id=(plane * NY + yh, col), device_id_type=MESH)
    others(greet)

    home = lax.div(row, 2)
    k_slot = lax.rem(row, 2) * NQ + col
    k_plane = lax.div(k_slot, 4)

    def k_source(n):
        return 2 * col + lax.div(z, 4), 4 * lax.rem(z, 4) + n

    def k_from_self(n):
        source_row, source_col = k_source(n)
        return (source_row == row) & (source_col == col)

    def k_to_self(n):
        return (k_plane == z) & (n == yh) & (home == col)

    def k_greet(n, carry):
        @pl.when(jnp.logical_not(k_from_self(n)))
        def _():
            pl.semaphore_signal(barrier, inc=1, device_id=k_source(n), device_id_type=MESH)

        return carry

    lax.fori_loop(0, 4, k_greet, 0)

    inputs = [
        pltpu.make_async_copy(source, target, in_sem.at[n])
        for n, (source, target) in enumerate(
            (
                (w_attn_any, w_attn), (mask_any, mask_in), (chain_any, chain_in), (bias_any, chain_bias),
                (w_bias_any, bias_weights), (w_attn_out_any, w_attn_out),
            )
        )
    ]
    for copy in inputs:
        copy.start()

    def l_block(m):
        source_row, source_col = group_device(m)
        return lbuf.at[pl.ds(source_row * 16, 16), pl.ds(source_col * 128, 128)]

    def r_block(m):
        return rbuf.at[m]

    def l_copy(m, slot):
        return remote(lt.at[m], l_block(slot), l_send.at[m], l_recv.at[slot], *group_device(m))

    def r_copy(m, slot):
        return remote(rt.at[pl.ds(m * 2, 2)], r_block(slot), r_send.at[m], r_recv.at[slot], *group_device(m))

    l_own = pltpu.make_async_copy(lt.at[me], l_block(me), own_sem.at[0])
    r_own = pltpu.make_async_copy(rt.at[pl.ds(me * 2, 2)], r_block(me), own_sem.at[4])
    l_own.start()
    r_own.start()

    proj_in[...] = jnp.zeros_like(proj_in)
    wo_msg[...] = jnp.zeros_like(wo_msg)
    qg_msg[...] = jnp.zeros_like(qg_msg)
    single_norm = layer_norm(single[...].astype(jnp.float32), -1).astype(jnp.bfloat16)

    remaining = k_to_self(yh)
    pl.semaphore_wait(barrier, GROUP + 5 - remaining.astype(jnp.int32))
    others(lambda m: r_copy(m, me).start(), 1, 9)
    others(lambda m: l_copy(m, me).start())
    others(lambda m: r_copy(m, me).start(), 9, EARLY)

    for copy in inputs:
        copy.wait()
    for place, which in enumerate((1, 2, 0, 3)):
        proj_in[place * SLOT : place * SLOT + HEAD_DIM, :] = w_attn[which].astype(jnp.float32)
    proj = proj_in[...].astype(jnp.bfloat16)
    key_value = dot(proj[0 : 2 * SLOT], single_norm, 1, 1)
    square[0:SLOT, 0:64] = key_value[0:SLOT]
    square[0:SLOT, 64:128] = key_value[SLOT : 2 * SLOT]
    square[HEAD_DIM : HEAD_DIM + 1, 0:64] = mask_in[...].astype(jnp.float32)
    square[HEAD_DIM : HEAD_DIM + 1, 64:128] = chain_in[...].astype(jnp.float32)
    kv_msg[...] = square[0:SLOT, :].astype(jnp.bfloat16)
    first_rows = dot(single_norm[0:16], proj[2 * SLOT : 4 * SLOT], 1, 1)[0:8]
    scaled = (first_rows * (HEAD_DIM ** (-0.5))).astype(jnp.bfloat16).astype(jnp.float32)
    lane = lax.broadcasted_iota(jnp.int32, (8, 2 * SLOT), 1)
    qg_msg[:, 0 : 2 * SLOT] = jnp.where(lane < SLOT, scaled, jax.nn.sigmoid(first_rows))

    k_own = pltpu.make_async_copy(kv_msg, kv_all.at[k_slot], own_sem.at[1])

    def k_copy(n, slot):
        return remote(kv_msg, kv_all.at[slot], k_send.at[n], k_recv.at[lax.rem(slot, 4)], k_plane * NY + n, home)

    def k_start(n, carry):
        stays = k_to_self(n)

        @pl.when(stays)
        def _():
            k_own.start()

        @pl.when(jnp.logical_not(stays))
        def _():
            k_copy(n, k_slot).start()

        return carry

    lax.fori_loop(0, 4, k_start, 0)

    def q_copy(target, slot):
        return remote(qg_msg, qg_all.at[slot], q_send.at[target], q_recv.at[slot], row, target)

    q_own = pltpu.make_async_copy(qg_msg, qg_all.at[col], own_sem.at[2])
    q_own.start()

    def q_start(n, carry):
        target = lax.rem(col + n, NQ)
        q_copy(target, col).start()
        return carry

    lax.fori_loop(1, NQ, q_start, 0)
    others(lambda m: r_copy(m, me).start(), EARLY, GROUP)

    l_own.wait()
    others(lambda m: l_copy(m, m).wait_recv())

    def z_copy(plane, way, target_z):
        block = lbuf.at[pl.ds(plane * 64, 64), :]
        return remote(block, block, z_send.at[way, plane], z_recv.at[plane], target_z * NY + yh, col)

    def kz_copy(plane, way, target_z):
        block = kv_all.at[pl.ds(plane * 4, 4)]
        return remote(block, block, kz_send.at[way, plane], kz_recv.at[plane], target_z * NY + yh, col)

    def plane_at(offset):
        return lax.rem(z + NZ + offset, NZ)

    def k_wait(n, carry):
        from_self = k_from_self(n)

        @pl.when(from_self)
        def _():
            k_own.wait()

        @pl.when(jnp.logical_not(from_self))
        def _():
            k_copy(0, z * 4 + n).wait_recv()

        return carry

    lax.fori_loop(0, 4, k_wait, 0)

    def ring_step(step):
        for copy in (z_copy, kz_copy):
            if step:
                copy(plane_at(-step), 0, up).wait_recv()
            copy(plane_at(-step), 0, up).start()
            if step < 3:
                if step:
                    copy(plane_at(step), 1, down).wait_recv()
                copy(plane_at(step), 1, down).start()

    ring_step(0)

    proj_in[0:SLOT, :] = jnp.zeros((SLOT, 384), jnp.float32)
    proj_in[0:HEAD_DIM, :] = w_attn_out[...].astype(jnp.float32)
    wo_msg[...] = proj_in[0:SLOT, :].astype(jnp.bfloat16)
    square[...] = jnp.zeros_like(square)
    square[:, 0:HEADS] = jnp.broadcast_to(chain_bias[...], (128, HEADS))
    chain_heads = square[...].T[0:HEADS]

    ring_step(1)

    def gates(tile, carry):
        rows = pl.ds(pl.multiple_of(tile * 256, 256), 256)
        pair_norm = layer_norm(pair[rows, :].astype(jnp.float32), -1).astype(jnp.bfloat16)
        gate_tri[rows, :] = jax.nn.sigmoid(dot(pair_norm, w_gate[...], 1, 0))
        return carry

    lax.fori_loop(0, 4, gates, 0)

    ring_step(2)
    ring_step(3)
    for copy in (z_copy, kz_copy):
        copy(plane_at(4), 0, up).wait_recv()
        copy(plane_at(3), 1, down).wait_recv()
    q_own.wait()

    def q_wait(n, carry):
        target = lax.rem(col + n, NQ)
        q_copy(target, col).wait_send()
        q_copy(target, target).wait_recv()
        return carry

    lax.fori_loop(1, NQ, q_wait, 0)
    for head in range(HEADS):
        lanes = slice(head * SLOT, head * SLOT + SLOT)
        q_full[:, lanes] = qg_all[head, :, 0:SLOT]
        gate_full[:, lanes] = qg_all[head, :, SLOT : 2 * SLOT]


    low = kv_all[0:HEADS].astype(jnp.float32).reshape(WIDE, 128)
    high = kv_all[HEADS : 2 * HEADS].astype(jnp.float32).reshape(WIDE, 128)
    lane = lax.broadcasted_iota(jnp.int32, (WIDE, 128), 1)
    keys = jnp.where(lane < 64, low, pltpu.roll(high, 64, 1))
    values = jnp.where(lane < 64, pltpu.roll(low, 64, 1), high)
    mask_cols = keys[HEAD_DIM : HEAD_DIM + 1, :]
    chain_cols = values[HEAD_DIM : HEAD_DIM + 1, :]
    head_of_row = lax.broadcasted_iota(jnp.int32, (HEADS, WIDE), 0)
    lane_wide = lax.broadcasted_iota(jnp.int32, (HEADS, WIDE), 1)
    own_block = head_of_row == lax.div(lane_wide, SLOT)
    depth = lax.rem(lane_wide, SLOT)
    own_values = jnp.where(own_block & (depth < HEAD_DIM), 1.0, 0.0)
    own_sum = jnp.where(own_block & (depth == HEAD_DIM), 1.0, 0.0)
    spread = jnp.concatenate(
        [jnp.broadcast_to(q_full[i : i + 1, :], (HEADS, WIDE)) * own_values for i in range(8)], axis=0
    ).astype(jnp.bfloat16)
    same = jnp.concatenate(
        [
            chain_heads * jnp.where(chain_cols == chain_in[0:1, i : i + 1].astype(jnp.float32), 1.0, 0.0)
            for i in range(8)
        ],
        axis=0,
    )
    bias_all[...] = dot(spread, keys.astype(jnp.bfloat16), 1, 0) + same
    values_low[...] = values.astype(jnp.bfloat16)
    own_values_kept[...] = own_values
    own_sum_kept[...] = own_sum
    mask_kept[...] = mask_cols

    r_own.wait()
    others(lambda m: r_copy(m, m).wait_recv())

    def t_copy(m, slot):
        return remote(
            tsend.at[lax.rem(m, 2), lax.div(m, 2)], tin.at[slot], t_send.at[m], t_recv.at[slot],
            lax.div(m, 2), 2 * z + lax.rem(m, 2),
        )

    def t_stays(m):
        return (lax.div(m, 2) == row) & (2 * z + lax.rem(m, 2) == col)

    t_own = pltpu.make_async_copy(tsend.at[col % 2, row], tin.at[me], own_sem.at[5])

    def multiply(step, carry):
        tile = lax.rem(step + z, 2)
        rows = pl.ds(pl.multiple_of(tile * 256, 256), 256)
        sums = []
        for channel in range(2):
            total = jnp.zeros((256, 256), jnp.float32)
            for pair_of_q in range(NQ // 2):
                right = jnp.concatenate(
                    [
                        jnp.concatenate([rbuf[y * NQ + 2 * pair_of_q + n, channel] for y in range(NY)], axis=0)
                        for n in range(2)
                    ],
                    axis=1,
                )
                total = total + dot(lbuf[rows, pair_of_q * 256 : pair_of_q * 256 + 256], right, 1, 1)
            sums.append(total)
        channel = lax.rem(lax.div(lax.broadcasted_iota(jnp.int32, (256, 256), 0), 8), 2)
        both = jnp.where(channel == 0, sums[0], sums[1]).astype(jnp.bfloat16)
        for half in range(2):
            tsend[half, pl.ds(tile * 16, 16)] = both[:, half * 128 : half * 128 + 128].reshape(16, 16, 128)

        def t_start(n, inner):
            m = tile * 32 + lax.rem(me + n, 32)
            stays = t_stays(m)

            @pl.when(stays)
            def _():
                t_own.start()

            @pl.when(jnp.logical_not(stays))
            def _():
                t_copy(m, me).start()

            return inner

        lax.fori_loop(0, 32, t_start, 0)
        return carry

    lax.fori_loop(0, 2, multiply, 0)

    def w_copy(target, slot):
        return remote(wo_msg, wo_all.at[slot], w_send.at[target], w_recv.at[slot], row, target)

    w_own = pltpu.make_async_copy(wo_msg, wo_all.at[col], own_sem.at[3])
    w_own.start()

    def w_start(n, carry):
        w_copy(lax.rem(col + n, NQ), col).start()
        return carry

    lax.fori_loop(1, NQ, w_start, 0)

    others(lambda m: l_copy(m, me).wait_send())
    others(lambda m: r_copy(m, me).wait_send())
    for step in range(4):
        for copy in (z_copy, kz_copy):
            copy(plane_at(-step), 0, up).wait_send()
            if step < 3:
                copy(plane_at(step), 1, down).wait_send()

    def k_sent(n, carry):
        @pl.when(jnp.logical_not(k_to_self(n)))
        def _():
            k_copy(n, k_slot).wait_send()

        return carry

    lax.fori_loop(0, 4, k_sent, 0)

    def t_wait(s, carry):
        from_self = (col // 2 == z) & (s == me)

        @pl.when(from_self)
        def _():
            t_own.wait()

        @pl.when(jnp.logical_not(from_self))
        def _():
            t_copy(s, s).wait_recv()

        return carry

    lax.fori_loop(0, GROUP, t_wait, 0)

    tin32[...] = tin[...].astype(jnp.float32).reshape(1024, 128)

    hidden = w_down.shape[0]

    def pair_step(step, carry):
        rows = pl.ds(pl.multiple_of(step * 256, 256), 256)
        updates = []
        for inner in range(2):
            block = tin32[pl.ds(step * 2 + inner, 128, stride=8), :]
            updates.append(dot(layer_norm(block, 0).astype(jnp.bfloat16), w_out[...], 0, 0))
        update = jnp.concatenate(updates, axis=0)
        pair_mid = pair[rows, :].astype(jnp.float32) + gate_tri[rows, :] * update
        trans_in = layer_norm(pair_mid, -1).astype(jnp.bfloat16)
        both_parts = dot(trans_in, w_in[...], 1, 0)
        gate_part = both_parts[:, :hidden]
        act = (gate_part / (1.0 + jnp.exp(-gate_part)) * both_parts[:, hidden:]).astype(jnp.bfloat16)
        new_pair = (pair_mid + dot(act, w_down[...], 1, 0)).astype(jnp.bfloat16)
        pair_out[rows, :] = new_pair
        bias_norm = layer_norm(new_pair.astype(jnp.float32), -1).astype(jnp.bfloat16)
        linear = dot(bias_weights[...], bias_norm, 1, 1)
        for inner in range(2):
            place = pl.multiple_of(step * 32 + inner * 16, 16)
            bias_all[pl.ds(place, 16), :] += linear[:, inner * 128 : inner * 128 + 128]
        return carry

    lax.fori_loop(0, 4, pair_step, 0)

    weights = jnp.exp(bias_all[...]) * mask_kept[...]
    denominator = jnp.sum(weights, axis=1, keepdims=True)
    products = dot(weights.astype(jnp.bfloat16), values_low[...], 1, 1)
    for i in range(8):
        span = slice(i * HEADS, i * HEADS + HEADS)
        kept = products[span] * own_values_kept[...] + denominator[span] * own_sum_kept[...]
        part[i : i + 1, :] = jnp.sum(kept, axis=0, keepdims=True)

    def p_copy(target, slot):
        return remote(part, parts.at[slot], p_send.at[target], p_recv.at[slot], row, target)

    def p_start(n, carry):
        p_copy(lax.rem(col + n, NQ), col).start()
        return carry

    lax.fori_loop(1, NQ, p_start, 0)
    p_own = pltpu.make_async_copy(part, parts.at[col], own_sem.at[6])
    p_own.start()

    def t_sent(m, carry):
        @pl.when(jnp.logical_not(t_stays(m)))
        def _():
            t_copy(m, me).wait_send()

        return carry

    lax.fori_loop(0, GROUP, t_sent, 0)
    w_own.wait()

    def w_wait(n, carry):
        target = lax.rem(col + n, NQ)
        w_copy(target, target).wait_recv()
        w_copy(target, col).wait_send()
        return carry

    lax.fori_loop(1, NQ, w_wait, 0)
    out_weights = wo_all[...].reshape(WIDE, 384)
    p_own.wait()

    def p_wait(n, carry):
        target = lax.rem(col + n, NQ)
        p_copy(target, target).wait_recv()
        p_copy(target, col).wait_send()
        return carry

    lax.fori_loop(1, NQ, p_wait, 0)
    total = parts[0]
    for n in range(1, NQ):
        total = total + parts[n]
    lane = lax.rem(lax.broadcasted_iota(jnp.int32, (8, WIDE), 1), SLOT)
    below = jnp.where(lane == HEAD_DIM, total, 0.0)
    for shift in (1, 2, 4, 8, 16):
        below = below + pltpu.roll(below, WIDE - shift, 1)
    gated = (gate_full[...] * (total / below)).astype(jnp.bfloat16)
    mixed = dot(gated, out_weights, 1, 0)
    single_out[...] = (single[0:8, :].astype(jnp.float32) + mixed).astype(jnp.bfloat16)


def block(lt, rt, *rest):
    dma = pltpu.SemaphoreType.DMA
    vmem = pl.BlockSpec(memory_space=pltpu.VMEM)
    anywhere = pl.BlockSpec(memory_space=pl.ANY)
    return pl.pallas_call(
        block_kernel,
        out_shape=(
            jax.ShapeDtypeStruct((1024, 128), jnp.bfloat16),
            jax.ShapeDtypeStruct((8, 384), jnp.bfloat16),
        ),
        in_specs=[anywhere] * 2 + [vmem] * 6 + [anywhere] * 6,
        out_specs=(vmem, vmem),
        scratch_shapes=[
            pltpu.VMEM((512, 2048), jnp.bfloat16),
            pltpu.VMEM((GROUP, 2, 64, 128), jnp.bfloat16),
            pltpu.VMEM((2, 32, 16, 128), jnp.bfloat16),
            pltpu.VMEM((GROUP, 16, 128), jnp.bfloat16),
            pltpu.VMEM((1024, 128), jnp.float32),
            pltpu.VMEM((1024, 128), jnp.float32),
            pltpu.VMEM((SLOT, 128), jnp.bfloat16),
            pltpu.VMEM((2 * NQ, SLOT, 128), jnp.bfloat16),
            pltpu.VMEM((8, 128), jnp.float32),
            pltpu.VMEM((NQ, 8, 128), jnp.float32),
            pltpu.VMEM((SLOT, 384), jnp.bfloat16),
            pltpu.VMEM((NQ, SLOT, 384), jnp.bfloat16),
            pltpu.VMEM((128, 384), jnp.float32),
            pltpu.VMEM((128, 128), jnp.float32),
            pltpu.VMEM((8, WIDE), jnp.float32),
            pltpu.VMEM((8, WIDE), jnp.float32),
            pltpu.VMEM((128, 128), jnp.float32),
            pltpu.VMEM((8, WIDE), jnp.float32),
            pltpu.VMEM((NQ, 8, WIDE), jnp.float32),
            pltpu.VMEM((1, 64), jnp.int32),
            pltpu.VMEM((1, 64), jnp.int32),
            pltpu.VMEM((1, HEADS), jnp.float32),
            pltpu.VMEM((HEADS, 128), jnp.bfloat16),
            pltpu.VMEM((4, HEAD_DIM, 384), jnp.bfloat16),
            pltpu.VMEM((HEAD_DIM, 384), jnp.bfloat16),
            pltpu.VMEM((WIDE, 128), jnp.bfloat16),
            pltpu.VMEM((HEADS, WIDE), jnp.float32),
            pltpu.VMEM((HEADS, WIDE), jnp.float32),
            pltpu.VMEM((1, 128), jnp.float32),
            dma((7,)),
            dma((6,)),
            dma((GROUP,)),
            dma((GROUP,)),
            dma((GROUP,)),
            dma((GROUP,)),
            dma((2, NZ)),
            dma((NZ,)),
            dma((4,)),
            dma((4,)),
            dma((2, NZ)),
            dma((NZ,)),
            dma((NQ,)),
            dma((NQ,)),
            dma((NQ,)),
            dma((NQ,)),
            dma((GROUP,)),
            dma((GROUP,)),
            dma((NQ,)),
            dma((NQ,)),
        ],
        compiler_params=pltpu.CompilerParams(
            collective_id=0, has_side_effects=True, vmem_limit_bytes=40 * 1024 * 1024
        ),
        name="pairformer",
    )(lt, rt, *rest)


def local(
    pair,
    panel_left,
    panel_right,
    single,
    token_mask,
    chain_ids,
    w_tri_gate,
    w_tri_out,
    w_trans_in,
    w_trans_down,
    w_bias,
    chain_bias,
    w_attn,
    w_attn_out,
):
    lt = jnp.transpose(panel_left, (2, 0, 1)).reshape(GROUP, 16, 128)
    rt = jnp.transpose(panel_right, (2, 0, 1))
    pair_out, single_out = block(
        lt,
        rt,
        pair.reshape(1024, 128),
        single,
        w_tri_gate,
        w_tri_out,
        w_trans_in,
        w_trans_down,
        token_mask.reshape(1, 64),
        chain_ids.reshape(1, 64),
        chain_bias.reshape(1, HEADS),
        jnp.transpose(w_bias),
        jnp.transpose(w_attn, (0, 2, 1)),
        w_attn_out,
    )
    return (pair_out.reshape(8, 128, 128), single_out)


def solution(mesh):
    in_specs = (
        P("row", "col", None),
        P("row", "col", None),
        P("row", "col", None),
        P("row", None),
        P("row"),
        P("row"),
        P(),
        P(),
        P(),
        P(),
        P(),
        P(),
        P(None, None, "col"),
        P("col", None),
    )
    out_specs = (P("row", "col", None), P("row", None))
    return jax.shard_map(local, mesh=mesh, in_specs=in_specs, out_specs=out_specs, check_vma=False)
```

time: 440 us -> 131 us (0.30)
  blocking collectives: 262 us -> 0 us
  Pallas kernels: 0 us -> 124 us
  waiting for transfers between devices: 82 us -> 0 us
  starting transfers between devices: 34.2 us -> 0 us
  local copies, waits for them, and re-layouts: 25.9 us -> 5.88 us
  between operations: 16.6 us -> 0.84 us
  matrix products: 10.5 us -> 0 us
  other arithmetic: 5.78 us -> 0 us
    unnamed x1 -> x0, blocking collectives: 145 us -> none
    pallas_call x0 -> x1, Pallas kernels: none -> 124 us  [block(): pl.pallas_call(block_kernel, out_shape=(jax.ShapeDtypeStruct((1024, 128),...]
    all_to_all x4 -> x0, waiting for transfers between devices: 81.4 us -> none  [the longest x1 63.5 us: local(): lax.all_to_all(right_first, 'row', split_axis=0, concat_axis=1, tiled=True)]
    psum x1 -> x0, blocking collectives: 68.6 us -> none  [local(): numerator, denominator = lax.psum((numerator_part, denominator_part), 'col')]
    all_gather x1 -> x0, blocking collectives: 48.1 us -> none  [local(): out_full = lax.all_gather(w_attn_out, 'col', axis=0, tiled=True)]
    all_to_all x4 -> x0, starting transfers between devices: 34.1 us -> none  [the longest x1 16.5 us: local(): lax.all_to_all(left_first, 'row', split_axis=0, concat_axis=1, tiled=True)]
    all_to_all x4 -> x0, local copies, waits for them, and re-layouts: 13.3 us -> none  [the longest x2 10.9 us: local(): lax.all_to_all(right_first, 'row', split_axis=0, concat_axis=1, tiled=True)]
    dot_general x11 -> x0, matrix products: 10.5 us -> none  [the longest x1 4.15 us: local(): lax.dot_general(lax.all_gather(left_moved, 'col', axis=2, tiled=True), ri...]
  transfers between devices with their start and end apart: 7 -> 0, of which waited for: 3 -> 0; matrix products, arithmetic and copies ran while one was open for 7% -> 0% of each run, Pallas kernels for 0% -> 0%
where the time goes in v2:
time: 131 us; the launch traced here: 130 us
  Pallas kernels  124 us (95%)
  local copies, waits for them, and re-layouts  5.88 us (4%)
    pallas_call x1, Pallas kernels, block(): pl.pallas_call(block_kernel, out_shape=(jax.ShapeDtypeStruct((1024, 128),...  124 us
    unnamed x27, local copies, waits for them, and re-layouts  4.75 us

profile of v2, /device:TPU:1, one launch (start us, length us, event | category | flops | bytes accessed | tf_op | source)
XLA Modules:
  0.0 130.5 jit_solution(17339560723594744301)
XLA Ops:
  0.6 1.1 copy.16
  1.8 0.0 copy-start
  1.8 0.0 copy-start.1
  1.8 0.0 copy-start.2
  1.8 0.0 copy-start.3
  1.8 0.0 copy-start.4
  1.8 0.0 copy-start.5
  1.8 0.0 copy-start.6
  1.9 0.0 copy-start.7
  1.9 0.0 copy-start.8
  1.9 0.0 copy-start.9
  1.9 0.0 copy-start.10
  1.9 0.0 copy-start.11
  1.9 3.4 %copy.17 = bf16[64,128,128]{1,0,2:T(8,128)(2,1)S(1)} copy(bf16[64,128,128]{2,1,0:T(8,128)(2,1)} %param.16) | data formatting | bytes 4194304 | tf_op args[2]
  5.3 0.0 copy-done
  5.3 0.0 copy-done.1
  5.3 0.0 copy-done.2
  5.3 0.0 copy-done.3
  5.3 0.0 copy-done.4
  5.3 0.0 copy-done.5
  5.4 0.0 copy-done.6
  5.4 123.8 %pairformer.1 = (bf16[1024,128]{1,0:T(8,128)(2,1)S(1)}, bf16[8,384]{1,0:T(8,128)(2,1)S(1)}) custom-call(bf16[64,16,128]{2,1,0:T(8,128)(2,1)S(1)} %bitcast.11, bf16[128,64,128]{2,1,0:T(8,128)(2,1)S(1)} %bitcast.10, bf16[1024,128]{1,0:T(8,128)(2,1)S(1)} %bitcast.12, bf16[64,384]{1,0:T(8,128)(2,1)S(1)} %copy-done.4, bf16[128,128]{1,0:T(8,128)(2,1)S(1)} %copy-done.5, ...), custom_call_target="tpu_custom_call" | custom-call | tf_op jit(solution)/shard_map/pairformer/pallas_call | solution.py:483
  129.2 0.7 copy.20
  129.9 0.6 copy.21
  (5 shorter events, 0.0 us)
Async XLA Ops:
  1.8 3.5 %copy-start = (bf16[8,128,128]{2,1,0:T(8,128)(2,1)S(1)}, bf16[8,128,128]{2,1,0:T(8,128)(2,1)}, u32[]{:S(2)}) copy-start(bf16[8,128,128]{2,1,0:T(8,128)(2,1)} %param.14) | copy-start | bytes 786436
  1.8 3.5 %copy-start.1 = (bf16[128,1024]{1,0:T(8,128)(2,1)S(1)}, bf16[128,1024]{1,0:T(8,128)(2,1)}, u32[]{:S(2)}) copy-start(bf16[128,1024]{1,0:T(8,128)(2,1)} %w_in.1) | copy-start | bytes 786436
  1.8 3.5 %copy-start.2 = (bf16[512,128]{1,0:T(8,128)(2,1)S(1)}, bf16[512,128]{1,0:T(8,128)(2,1)}, u32[]{:S(2)}) copy-start(bf16[512,128]{1,0:T(8,128)(2,1)} %w_down.1) | copy-start | bytes 393220
  1.8 3.5 %copy-start.3 = (bf16[4,384,24]{1,2,0:T(8,128)(2,1)S(1)}, bf16[4,384,24]{1,2,0:T(8,128)(2,1)}, u32[]{:S(2)}) copy-start(bf16[4,384,24]{1,2,0:T(8,128)(2,1)} %param.26) | copy-start | bytes 221188
  1.8 3.5 %copy-start.4 = (bf16[64,384]{1,0:T(8,128)(2,1)S(1)}, bf16[64,384]{1,0:T(8,128)(2,1)}, u32[]{:S(2)}) copy-start(bf16[64,384]{1,0:T(8,128)(2,1)} %single.1) | copy-start | bytes 147460
  1.8 3.5 %copy-start.5 = (bf16[128,128]{1,0:T(8,128)(2,1)S(1)}, bf16[128,128]{1,0:T(8,128)(2,1)}, u32[]{:S(2)}) copy-start(bf16[128,128]{1,0:T(8,128)(2,1)} %w_gate.1) | copy-start | bytes 98308
  1.8 3.5 %copy-start.6 = (bf16[128,128]{1,0:T(8,128)(2,1)S(1)}, bf16[128,128]{1,0:T(8,128)(2,1)}, u32[]{:S(2)}) copy-start(bf16[128,128]{1,0:T(8,128)(2,1)} %w_out.1) | copy-start | bytes 98308
  1.9 3.5 %copy-start.7 = (bf16[24,384]{1,0:T(8,128)(2,1)S(1)}, bf16[24,384]{1,0:T(8,128)(2,1)}, u32[]{:S(2)}) copy-start(bf16[24,384]{1,0:T(8,128)(2,1)} %w_attn_out_any.1) | copy-start | bytes 55300
  1.9 3.5 %copy-start.8 = (bf16[128,16]{0,1:T(8,128)(2,1)S(1)}, bf16[128,16]{0,1:T(8,128)(2,1)}, u32[]{:S(2)}) copy-start(bf16[128,16]{0,1:T(8,128)(2,1)} %param.24) | copy-start | bytes 12292
  1.9 3.5 %copy-start.9 = (s32[64]{0:T(128)S(1)}, s32[64]{0:T(128)}, u32[]{:S(2)}) copy-start(s32[64]{0:T(128)} %param.18) | copy-start | bytes 772
  1.9 3.5 %copy-start.10 = (s32[64]{0:T(128)S(1)}, s32[64]{0:T(128)}, u32[]{:S(2)}) copy-start(s32[64]{0:T(128)} %param.19) | copy-start | bytes 772
  1.9 3.5 %copy-start.11 = (f32[16]{0:T(128)S(1)}, f32[16]{0:T(128)}, u32[]{:S(2)}) copy-start(f32[16]{0:T(128)} %param.25) | copy-start | bytes 196

commit v3 on v2

--- a/solution.py
+++ b/solution.py
@@ -14,7 +14,9 @@
 SLOT = 32
 WIDE = HEADS * SLOT
 MESH = pl.DeviceIdType.MESH
-EARLY = 24
+EARLY = 48
+CHUNK = 16
+CHUNKS = 4
 
 epsilon = 1e-05
 
@@ -37,12 +39,13 @@
 
 
 def block_kernel(
-    lt, rt, pair, single, w_gate, w_out, w_in, w_down, mask_any, chain_any, bias_any, w_bias_any, w_attn_any, w_attn_out_any,
+    left_any, right_any, pair_any, single_any, w_gate_any, w_out_any, w_in_any, w_down_any, mask_any, chain_any, bias_any, w_bias_any, w_attn_any, w_attn_out_any,
     pair_out, single_out,
-    lbuf, rbuf, tsend, tin, tin32, gate_tri, kv_msg, kv_all, qg_msg, qg_all, wo_msg, wo_all, proj_in, square,
+    left_in, right_in, lt, rt, lbuf, rbuf, tsend, tin, tin32, gate_tri, kv_msg, kv_all, qg_msg, qg_all, wo_msg, wo_all, proj_in, square,
     q_full, gate_full, bias_all, part, parts, mask_in, chain_in, chain_bias, bias_weights, w_attn, w_attn_out,
     values_low, own_values_kept, own_sum_kept, mask_kept,
-    own_sem, in_sem, l_send, l_recv, r_send, r_recv, z_send, z_recv, k_send, k_recv, kz_send, kz_recv,
+    pair, single, w_gate, w_out, w_in, w_down,
+    own_sem, in_sem, panel_sem, l_send, l_recv, r_send, r_recv, z_send, z_recv, k_send, k_recv, kz_send, kz_recv,
     q_send, q_recv, w_send, w_recv, t_send, t_recv, p_send, p_recv,
 ):
     row = lax.axis_index("row")
@@ -68,9 +71,21 @@
     def greet(m):
         pl.semaphore_signal(barrier, inc=1, device_id=group_device(m), device_id_type=MESH)
 
+    left_copy = pltpu.make_async_copy(left_any, left_in, panel_sem.at[CHUNKS])
+    left_copy.start()
+    single_copy = pltpu.make_async_copy(single_any, single, own_sem.at[7])
+    single_copy.start()
+
+    def right_copy(chunk):
+        rows = pl.ds(pl.multiple_of(chunk * CHUNK, CHUNK), CHUNK)
+        return pltpu.make_async_copy(right_any.at[rows], right_in.at[rows], panel_sem.at[chunk])
+
+    for chunk in range(CHUNKS):
+        right_copy(chunk).start()
     for plane in (up, down):
         pl.semaphore_signal(barrier, inc=1, device_id=(plane * NY + yh, col), device_id_type=MESH)
-    others(greet)
+    for n in range(61, GROUP):
+        greet(lax.rem(me + n, GROUP))
 
     home = lax.div(row, 2)
     k_slot = lax.rem(row, 2) * NQ + col
@@ -100,7 +115,8 @@
         for n, (source, target) in enumerate(
             (
                 (w_attn_any, w_attn), (mask_any, mask_in), (chain_any, chain_in), (bias_any, chain_bias),
-                (w_bias_any, bias_weights), (w_attn_out_any, w_attn_out),
+                (w_bias_any, bias_weights), (w_attn_out_any, w_attn_out), (w_gate_any, w_gate), (pair_any, pair),
+                (w_out_any, w_out), (w_in_any, w_in), (w_down_any, w_down),
             )
         )
     ]
@@ -117,8 +133,25 @@
     def l_copy(m, slot):
         return remote(lt.at[m], l_block(slot), l_send.at[m], l_recv.at[slot], *group_device(m))
 
-    def r_copy(m, slot):
-        return remote(rt.at[pl.ds(m * 2, 2)], r_block(slot), r_send.at[m], r_recv.at[slot], *group_device(m))
+    def r_copy(channel, m, slot):
+        return remote(
+            rt.at[m * 2 + channel], rbuf.at[slot, channel], r_send.at[channel, m], r_recv.at[channel, slot],
+            *group_device(m),
+        )
+
+    left_copy.wait()
+    lt[...] = jnp.transpose(left_in[...].astype(jnp.float32), (2, 0, 1)).reshape(GROUP, 16, 128).astype(jnp.bfloat16)
+
+    def turn(chunk, carry):
+        right_copy(chunk).wait()
+        for n in range(1, 16):
+            if n < 60 // CHUNKS + 1:
+                greet(lax.rem(me + chunk * (60 // CHUNKS) + n, GROUP))
+        rows = pl.ds(pl.multiple_of(chunk * CHUNK, CHUNK), CHUNK)
+        rt[:, rows, :] = jnp.transpose(right_in[rows], (2, 0, 1))
+        return carry
+
+    lax.fori_loop(0, CHUNKS, turn, 0)
 
     l_own = pltpu.make_async_copy(lt.at[me], l_block(me), own_sem.at[0])
     r_own = pltpu.make_async_copy(rt.at[pl.ds(me * 2, 2)], r_block(me), own_sem.at[4])
@@ -128,13 +161,14 @@
     proj_in[...] = jnp.zeros_like(proj_in)
     wo_msg[...] = jnp.zeros_like(wo_msg)
     qg_msg[...] = jnp.zeros_like(qg_msg)
+    single_copy.wait()
     single_norm = layer_norm(single[...].astype(jnp.float32), -1).astype(jnp.bfloat16)
 
     remaining = k_to_self(yh)
     pl.semaphore_wait(barrier, GROUP + 5 - remaining.astype(jnp.int32))
-    others(lambda m: r_copy(m, me).start(), 1, 9)
+    others(lambda m: r_copy(0, m, me).start(), 1, 9)
     others(lambda m: l_copy(m, me).start())
-    others(lambda m: r_copy(m, me).start(), 9, EARLY)
+    others(lambda m: r_copy(0, m, me).start(), 9, EARLY)
 
     for copy in inputs:
         copy.wait()
@@ -184,48 +218,8 @@
         return carry
 
     lax.fori_loop(1, NQ, q_start, 0)
-    others(lambda m: r_copy(m, me).start(), EARLY, GROUP)
-
-    l_own.wait()
-    others(lambda m: l_copy(m, m).wait_recv())
-
-    def z_copy(plane, way, target_z):
-        block = lbuf.at[pl.ds(plane * 64, 64), :]
-        return remote(block, block, z_send.at[way, plane], z_recv.at[plane], target_z * NY + yh, col)
-
-    def kz_copy(plane, way, target_z):
-        block = kv_all.at[pl.ds(plane * 4, 4)]
-        return remote(block, block, kz_send.at[way, plane], kz_recv.at[plane], target_z * NY + yh, col)
-
-    def plane_at(offset):
-        return lax.rem(z + NZ + offset, NZ)
-
-    def k_wait(n, carry):
-        from_self = k_from_self(n)
-
-        @pl.when(from_self)
-        def _():
-            k_own.wait()
-
-        @pl.when(jnp.logical_not(from_self))
-        def _():
-            k_copy(0, z * 4 + n).wait_recv()
-
-        return carry
-
-    lax.fori_loop(0, 4, k_wait, 0)
-
-    def ring_step(step):
-        for copy in (z_copy, kz_copy):
-            if step:
-                copy(plane_at(-step), 0, up).wait_recv()
-            copy(plane_at(-step), 0, up).start()
-            if step < 3:
-                if step:
-                    copy(plane_at(step), 1, down).wait_recv()
-                copy(plane_at(step), 1, down).start()
-
-    ring_step(0)
+    others(lambda m: r_copy(0, m, me).start(), EARLY, GROUP)
+    others(lambda m: r_copy(1, m, me).start())
 
     proj_in[0:SLOT, :] = jnp.zeros((SLOT, 384), jnp.float32)
     proj_in[0:HEAD_DIM, :] = w_attn_out[...].astype(jnp.float32)
@@ -234,8 +228,6 @@
     square[:, 0:HEADS] = jnp.broadcast_to(chain_bias[...], (128, HEADS))
     chain_heads = square[...].T[0:HEADS]
 
-    ring_step(1)
-
     def gates(tile, carry):
         rows = pl.ds(pl.multiple_of(tile * 256, 256), 256)
         pair_norm = layer_norm(pair[rows, :].astype(jnp.float32), -1).astype(jnp.bfloat16)
@@ -244,11 +236,106 @@
 
     lax.fori_loop(0, 4, gates, 0)
 
-    ring_step(2)
-    ring_step(3)
-    for copy in (z_copy, kz_copy):
+    l_own.wait()
+    others(lambda m: l_copy(m, m).wait_recv())
+
+    def z_copy(plane, way, target_z):
+        block = lbuf.at[pl.ds(plane * 64, 64), :]
+        return remote(block, block, z_send.at[way, plane], z_recv.at[plane], target_z * NY + yh, col)
+
+    def kz_copy(plane, way, target_z):
+        block = kv_all.at[pl.ds(plane * 4, 4)]
+        return remote(block, block, kz_send.at[way, plane], kz_recv.at[plane], target_z * NY + yh, col)
+
+    def plane_at(offset):
+        return lax.rem(z + NZ + offset, NZ)
+
+    def ring_step(copy, step):
+        if step:
+            copy(plane_at(-step), 0, up).wait_recv()
+        copy(plane_at(-step), 0, up).start()
+        if step < 3:
+            if step:
+                copy(plane_at(step), 1, down).wait_recv()
+            copy(plane_at(step), 1, down).start()
+
+    def ring_end(copy):
         copy(plane_at(4), 0, up).wait_recv()
         copy(plane_at(3), 1, down).wait_recv()
+
+    for step in range(4):
+        ring_step(z_copy, step)
+    ring_end(z_copy)
+
+    r_own.wait()
+
+    def t_copy(channel, m, slot):
+        return remote(
+            tsend.at[channel, lax.rem(m, 2), lax.div(m, 2)], tin.at[slot, channel],
+            t_send.at[channel, m], t_recv.at[channel, slot], lax.div(m, 2), 2 * z + lax.rem(m, 2),
+        )
+
+    def t_stays(m):
+        return (lax.div(m, 2) == row) & (2 * z + lax.rem(m, 2) == col)
+
+    def t_own(channel):
+        return pltpu.make_async_copy(tsend.at[channel, col % 2, row], tin.at[me, channel], own_sem.at[5 + channel])
+
+    for channel in range(2):
+        others(lambda m: r_copy(channel, m, m).wait_recv())
+
+        def multiply(step, carry):
+            tile = lax.rem(step + z, 2)
+            rows = pl.ds(pl.multiple_of(tile * 256, 256), 256)
+            total = jnp.zeros((256, 256), jnp.float32)
+            for pair_of_q in range(NQ // 2):
+                right = jnp.concatenate(
+                    [
+                        jnp.concatenate([rbuf[y * NQ + 2 * pair_of_q + n, channel] for y in range(NY)], axis=0)
+                        for n in range(2)
+                    ],
+                    axis=1,
+                )
+                total = total + dot(lbuf[rows, pair_of_q * 256 : pair_of_q * 256 + 256], right, 1, 1)
+            chosen = total.reshape(16, 2, 8, 256)[:, channel].astype(jnp.bfloat16)
+            for half in range(2):
+                tsend[channel, half, pl.ds(tile * 16, 16)] = chosen[:, :, half * 128 : half * 128 + 128]
+
+            def t_start(n, inner):
+                m = tile * 32 + lax.rem(me + n, 32)
+                stays = t_stays(m)
+
+                @pl.when(stays)
+                def _():
+                    t_own(channel).start()
+
+                @pl.when(jnp.logical_not(stays))
+                def _():
+                    t_copy(channel, m, me).start()
+
+                return inner
+
+            lax.fori_loop(0, 32, t_start, 0)
+            return carry
+
+        lax.fori_loop(0, 2, multiply, 0)
+
+    def k_wait(n, carry):
+        from_self = k_from_self(n)
+
+        @pl.when(from_self)
+        def _():
+            k_own.wait()
+
+        @pl.when(jnp.logical_not(from_self))
+        def _():
+            k_copy(0, z * 4 + n).wait_recv()
+
+        return carry
+
+    lax.fori_loop(0, 4, k_wait, 0)
+
+    ring_step(kz_copy, 0)
     q_own.wait()
 
     def q_wait(n, carry):
@@ -263,6 +350,29 @@
         q_full[:, lanes] = qg_all[head, :, 0:SLOT]
         gate_full[:, lanes] = qg_all[head, :, SLOT : 2 * SLOT]
 
+
+    ring_step(kz_copy, 1)
+
+    others(lambda m: l_copy(m, me).wait_send())
+    for channel in range(2):
+        others(lambda m: r_copy(channel, m, me).wait_send())
+    for step in range(4):
+        z_copy(plane_at(-step), 0, up).wait_send()
+        if step < 3:
+            z_copy(plane_at(step), 1, down).wait_send()
+
+    def k_sent(n, carry):
+        @pl.when(jnp.logical_not(k_to_self(n)))
+        def _():
+            k_copy(n, k_slot).wait_send()
+
+        return carry
+
+    lax.fori_loop(0, 4, k_sent, 0)
+
+    ring_step(kz_copy, 2)
+    ring_step(kz_copy, 3)
+    ring_end(kz_copy)
 
     low = kv_all[0:HEADS].astype(jnp.float32).reshape(WIDE, 128)
     high = kv_all[HEADS : 2 * HEADS].astype(jnp.float32).reshape(WIDE, 128)
@@ -293,59 +403,24 @@
     own_sum_kept[...] = own_sum
     mask_kept[...] = mask_cols
 
-    r_own.wait()
-    others(lambda m: r_copy(m, m).wait_recv())
-
-    def t_copy(m, slot):
-        return remote(
-            tsend.at[lax.rem(m, 2), lax.div(m, 2)], tin.at[slot], t_send.at[m], t_recv.at[slot],
-            lax.div(m, 2), 2 * z + lax.rem(m, 2),
-        )
-
-    def t_stays(m):
-        return (lax.div(m, 2) == row) & (2 * z + lax.rem(m, 2) == col)
-
-    t_own = pltpu.make_async_copy(tsend.at[col % 2, row], tin.at[me], own_sem.at[5])
-
-    def multiply(step, carry):
-        tile = lax.rem(step + z, 2)
-        rows = pl.ds(pl.multiple_of(tile * 256, 256), 256)
-        sums = []
-        for channel in range(2):
-            total = jnp.zeros((256, 256), jnp.float32)
-            for pair_of_q in range(NQ // 2):
-                right = jnp.concatenate(
-                    [
-                        jnp.concatenate([rbuf[y * NQ + 2 * pair_of_q + n, channel] for y in range(NY)], axis=0)
-                        for n in range(2)
-                    ],
-                    axis=1,
-                )
-                total = total + dot(lbuf[rows, pair_of_q * 256 : pair_of_q * 256 + 256], right, 1, 1)
-            sums.append(total)
-        channel = lax.rem(lax.div(lax.broadcasted_iota(jnp.int32, (256, 256), 0), 8), 2)
-        both = jnp.where(channel == 0, sums[0], sums[1]).astype(jnp.bfloat16)
-        for half in range(2):
-            tsend[half, pl.ds(tile * 16, 16)] = both[:, half * 128 : half * 128 + 128].reshape(16, 16, 128)
-
-        def t_start(n, inner):
-            m = tile * 32 + lax.rem(me + n, 32)
-            stays = t_stays(m)
-
-            @pl.when(stays)
+    for channel in range(2):
+
+        def t_wait(s, carry):
+            from_self = (col // 2 == z) & (s == me)
+
+            @pl.when(from_self)
             def _():
-                t_own.start()
-
-            @pl.when(jnp.logical_not(stays))
+                t_own(channel).wait()
+
+            @pl.when(jnp.logical_not(from_self))
             def _():
-                t_copy(m, me).start()
-
-            return inner
-
-        lax.fori_loop(0, 32, t_start, 0)
-        return carry
-
-    lax.fori_loop(0, 2, multiply, 0)
+                t_copy(channel, s, s).wait_recv()
+
+            return carry
+
+        lax.fori_loop(0, GROUP, t_wait, 0)
+
+    tin32[...] = tin[...].astype(jnp.float32).reshape(1024, 128)
 
     def w_copy(target, slot):
         return remote(wo_msg, wo_all.at[slot], w_send.at[target], w_recv.at[slot], row, target)
@@ -353,50 +428,17 @@
     w_own = pltpu.make_async_copy(wo_msg, wo_all.at[col], own_sem.at[3])
     w_own.start()
 
-    def w_start(n, carry):
-        w_copy(lax.rem(col + n, NQ), col).start()
-        return carry
-
-    lax.fori_loop(1, NQ, w_start, 0)
-
-    others(lambda m: l_copy(m, me).wait_send())
-    others(lambda m: r_copy(m, me).wait_send())
-    for step in range(4):
-        for copy in (z_copy, kz_copy):
-            copy(plane_at(-step), 0, up).wait_send()
-            if step < 3:
-                copy(plane_at(step), 1, down).wait_send()
-
-    def k_sent(n, carry):
-        @pl.when(jnp.logical_not(k_to_self(n)))
-        def _():
-            k_copy(n, k_slot).wait_send()
-
-        return carry
-
-    lax.fori_loop(0, 4, k_sent, 0)
-
-    def t_wait(s, carry):
-        from_self = (col // 2 == z) & (s == me)
-
-        @pl.when(from_self)
-        def _():
-            t_own.wait()
-
-        @pl.when(jnp.logical_not(from_self))
-        def _():
-            t_copy(s, s).wait_recv()
-
-        return carry
-
-    lax.fori_loop(0, GROUP, t_wait, 0)
-
-    tin32[...] = tin[...].astype(jnp.float32).reshape(1024, 128)
-
     hidden = w_down.shape[0]
 
     def pair_step(step, carry):
         rows = pl.ds(pl.multiple_of(step * 256, 256), 256)
+        for n in range(4):
+            offset = step * 4 + n
+
+            @pl.when(offset > 0)
+            def _():
+                w_copy(lax.rem(col + offset, NQ), col).start()
+
         updates = []
         for inner in range(2):
             block = tin32[pl.ds(step * 2 + inner, 128, stride=8), :]
@@ -434,13 +476,19 @@
         return carry
 
     lax.fori_loop(1, NQ, p_start, 0)
-    p_own = pltpu.make_async_copy(part, parts.at[col], own_sem.at[6])
+    p_own = pltpu.make_async_copy(part, parts.at[col], own_sem.at[8])
     p_own.start()
+
+    for step in range(4):
+        kz_copy(plane_at(-step), 0, up).wait_send()
+        if step < 3:
+            kz_copy(plane_at(step), 1, down).wait_send()
 
     def t_sent(m, carry):
         @pl.when(jnp.logical_not(t_stays(m)))
         def _():
-            t_copy(m, me).wait_send()
+            for channel in range(2):
+                t_copy(channel, m, me).wait_send()
 
         return carry
 
@@ -476,7 +524,7 @@
     single_out[...] = (single[0:8, :].astype(jnp.float32) + mixed).astype(jnp.bfloat16)
 
 
-def block(lt, rt, *rest):
+def block(*operands):
     dma = pltpu.SemaphoreType.DMA
     vmem = pl.BlockSpec(memory_space=pltpu.VMEM)
     anywhere = pl.BlockSpec(memory_space=pl.ANY)
@@ -486,13 +534,17 @@
             jax.ShapeDtypeStruct((1024, 128), jnp.bfloat16),
             jax.ShapeDtypeStruct((8, 384), jnp.bfloat16),
         ),
-        in_specs=[anywhere] * 2 + [vmem] * 6 + [anywhere] * 6,
+        in_specs=[anywhere] * 14,
         out_specs=(vmem, vmem),
         scratch_shapes=[
+            pltpu.VMEM((8, 128, 128), jnp.bfloat16),
+            pltpu.VMEM((64, 128, 128), jnp.bfloat16),
+            pltpu.VMEM((GROUP, 16, 128), jnp.bfloat16),
+            pltpu.VMEM((128, 64, 128), jnp.bfloat16),
             pltpu.VMEM((512, 2048), jnp.bfloat16),
             pltpu.VMEM((GROUP, 2, 64, 128), jnp.bfloat16),
-            pltpu.VMEM((2, 32, 16, 128), jnp.bfloat16),
-            pltpu.VMEM((GROUP, 16, 128), jnp.bfloat16),
+            pltpu.VMEM((2, 2, 32, 8, 128), jnp.bfloat16),
+            pltpu.VMEM((GROUP, 2, 8, 128), jnp.bfloat16),
             pltpu.VMEM((1024, 128), jnp.float32),
             pltpu.VMEM((1024, 128), jnp.float32),
             pltpu.VMEM((SLOT, 128), jnp.bfloat16),
@@ -518,12 +570,19 @@
             pltpu.VMEM((HEADS, WIDE), jnp.float32),
             pltpu.VMEM((HEADS, WIDE), jnp.float32),
             pltpu.VMEM((1, 128), jnp.float32),
-            dma((7,)),
-            dma((6,)),
+            pltpu.VMEM((1024, 128), jnp.bfloat16),
+            pltpu.VMEM((64, 384), jnp.bfloat16),
+            pltpu.VMEM((128, 128), jnp.bfloat16),
+            pltpu.VMEM((128, 128), jnp.bfloat16),
+            pltpu.VMEM((128, 1024), jnp.bfloat16),
+            pltpu.VMEM((512, 128), jnp.bfloat16),
+            dma((9,)),
+            dma((11,)),
+            dma((CHUNKS + 1,)),
             dma((GROUP,)),
             dma((GROUP,)),
-            dma((GROUP,)),
-            dma((GROUP,)),
+            dma((2, GROUP)),
+            dma((2, GROUP)),
             dma((2, NZ)),
             dma((NZ,)),
             dma((4,)),
@@ -534,16 +593,16 @@
             dma((NQ,)),
             dma((NQ,)),
             dma((NQ,)),
-            dma((GROUP,)),
-            dma((GROUP,)),
+            dma((2, GROUP)),
+            dma((2, GROUP)),
             dma((NQ,)),
             dma((NQ,)),
         ],
         compiler_params=pltpu.CompilerParams(
-            collective_id=0, has_side_effects=True, vmem_limit_bytes=40 * 1024 * 1024
+            collective_id=0, has_side_effects=True, vmem_limit_bytes=60 * 1024 * 1024
         ),
         name="pairformer",
-    )(lt, rt, *rest)
+    )(*operands)
 
 
 def local(
@@ -562,11 +621,9 @@
     w_attn,
     w_attn_out,
 ):
-    lt = jnp.transpose(panel_left, (2, 0, 1)).reshape(GROUP, 16, 128)
-    rt = jnp.transpose(panel_right, (2, 0, 1))
     pair_out, single_out = block(
-        lt,
-        rt,
+        panel_left,
+        panel_right,
         pair.reshape(1024, 128),
         single,
         w_tri_gate,

time: 131 us -> 115 us (0.88)
  Pallas kernels: 124 us -> 111 us
  local copies, waits for them, and re-layouts: 5.88 us -> 2.96 us
    pallas_call x1, Pallas kernels: 124 us -> 111 us  [block(): pl.pallas_call(block_kernel, out_shape=(jax.ShapeDtypeStruct((1024, 128),...]
    unnamed x27 -> x2, local copies, waits for them, and re-layouts: 4.75 us -> 2.96 us
where the time goes in v3:
time: 115 us
  Pallas kernels  111 us (97%)
  local copies, waits for them, and re-layouts  2.96 us (3%)
    pallas_call x1, Pallas kernels, block(): pl.pallas_call(block_kernel, out_shape=(jax.ShapeDtypeStruct((1024, 128),...  111 us
    unnamed x2, local copies, waits for them, and re-layouts  2.96 us

profile of v3, /device:TPU:1, one launch (start us, length us, event | category | flops | bytes accessed | tf_op | source)
XLA Modules:
  0.0 114.9 jit_solution(11555646906446260076)
XLA Ops:
  0.6 111.3 %pairformer.1 = (bf16[1024,128]{1,0:T(8,128)(2,1)}, bf16[8,384]{1,0:T(8,128)(2,1)}) custom-call(bf16[8,128,128]{2,1,0:T(8,128)(2,1)} %left_any.1, bf16[64,128,128]{2,1,0:T(8,128)(2,1)} %right_any.1, bf16[1024,128]{1,0:T(8,128)(2,1)} %bitcast.7, bf16[64,384]{1,0:T(8,128)(2,1)} %single_any.1, bf16[128,128]{1,0:T(8,128)(2,1)} %w_gate_any.1, ...), custom_call_target="tpu_custom_call" | custom-call | tf_op jit(solution)/shard_map/pairformer/pallas_call | solution.py:531
  111.9 1.7 %copy.18 = bf16[8,128,128]{2,1,0:T(8,128)(2,1)} copy(bf16[8,128,128]{2,1,0:T(8,128)(2,1)} %bitcast.8) | data formatting | bytes 524288
  113.6 1.3 %copy.19 = bf16[8,384]{1,0:T(8,128)(2,1)} copy(bf16[8,384]{1,0:T(8,128)(2,1)} %get-tuple-element.9) | data formatting | bytes 12288

commit v4 on v3

--- a/solution.py
+++ b/solution.py
@@ -131,11 +131,11 @@
         return rbuf.at[m]
 
     def l_copy(m, slot):
-        return remote(lt.at[m], l_block(slot), l_send.at[m], l_recv.at[slot], *group_device(m))
+        return remote(lt.at[m], l_block(slot), l_send, l_recv.at[slot], *group_device(m))
 
     def r_copy(channel, m, slot):
         return remote(
-            rt.at[m * 2 + channel], rbuf.at[slot, channel], r_send.at[channel, m], r_recv.at[channel, slot],
+            rt.at[m * 2 + channel], rbuf.at[slot, channel], r_send, r_recv.at[channel, slot],
             *group_device(m),
         )
 
@@ -267,12 +267,28 @@
         ring_step(z_copy, step)
     ring_end(z_copy)
 
+    def k_wait(n, carry):
+        from_self = k_from_self(n)
+
+        @pl.when(from_self)
+        def _():
+            k_own.wait()
+
+        @pl.when(jnp.logical_not(from_self))
+        def _():
+            k_copy(0, z * 4 + n).wait_recv()
+
+        return carry
+
+    lax.fori_loop(0, 4, k_wait, 0)
+
+    ring_step(kz_copy, 0)
     r_own.wait()
 
     def t_copy(channel, m, slot):
         return remote(
             tsend.at[channel, lax.rem(m, 2), lax.div(m, 2)], tin.at[slot, channel],
-            t_send.at[channel, m], t_recv.at[channel, slot], lax.div(m, 2), 2 * z + lax.rem(m, 2),
+            t_send, t_recv.at[channel, slot], lax.div(m, 2), 2 * z + lax.rem(m, 2),
         )
 
     def t_stays(m):
@@ -319,58 +335,23 @@
             return carry
 
         lax.fori_loop(0, 2, multiply, 0)
-
-    def k_wait(n, carry):
-        from_self = k_from_self(n)
-
-        @pl.when(from_self)
-        def _():
-            k_own.wait()
-
-        @pl.when(jnp.logical_not(from_self))
-        def _():
-            k_copy(0, z * 4 + n).wait_recv()
-
-        return carry
-
-    lax.fori_loop(0, 4, k_wait, 0)
-
-    ring_step(kz_copy, 0)
-    q_own.wait()
-
-    def q_wait(n, carry):
-        target = lax.rem(col + n, NQ)
-        q_copy(target, col).wait_send()
-        q_copy(target, target).wait_recv()
-        return carry
-
-    lax.fori_loop(1, NQ, q_wait, 0)
-    for head in range(HEADS):
-        lanes = slice(head * SLOT, head * SLOT + SLOT)
-        q_full[:, lanes] = qg_all[head, :, 0:SLOT]
-        gate_full[:, lanes] = qg_all[head, :, SLOT : 2 * SLOT]
-
-
-    ring_step(kz_copy, 1)
-
-    others(lambda m: l_copy(m, me).wait_send())
-    for channel in range(2):
-        others(lambda m: r_copy(channel, m, me).wait_send())
-    for step in range(4):
-        z_copy(plane_at(-step), 0, up).wait_send()
-        if step < 3:
-            z_copy(plane_at(step), 1, down).wait_send()
-
-    def k_sent(n, carry):
-        @pl.when(jnp.logical_not(k_to_self(n)))
-        def _():
-            k_copy(n, k_slot).wait_send()
-
-        return carry
-
-    lax.fori_loop(0, 4, k_sent, 0)
-
-    ring_step(kz_copy, 2)
+        if channel == 0:
+            ring_step(kz_copy, 1)
+            q_own.wait()
+
+            def q_wait(n, carry):
+                target = lax.rem(col + n, NQ)
+                q_copy(target, col).wait_send()
+                q_copy(target, target).wait_recv()
+                return carry
+
+            lax.fori_loop(1, NQ, q_wait, 0)
+            for head in range(HEADS):
+                lanes = slice(head * SLOT, head * SLOT + SLOT)
+                q_full[:, lanes] = qg_all[head, :, 0:SLOT]
+                gate_full[:, lanes] = qg_all[head, :, SLOT : 2 * SLOT]
+            ring_step(kz_copy, 2)
+
     ring_step(kz_copy, 3)
     ring_end(kz_copy)
 
@@ -484,15 +465,35 @@
         if step < 3:
             kz_copy(plane_at(step), 1, down).wait_send()
 
-    def t_sent(m, carry):
-        @pl.when(jnp.logical_not(t_stays(m)))
+    def sent(ref, sem):
+        remote(ref, ref, sem, own_sem.at[9], up * NY + yh, col).wait_send()
+
+    sent(lt.at[pl.ds(0, GROUP - 1)], l_send)
+    sent(rt.at[pl.ds(0, 2 * GROUP - 2)], r_send)
+    keeps_one = lax.div(col, 2) == z
+
+    @pl.when(keeps_one)
+    def _():
+        sent(tin.at[pl.ds(0, GROUP - 1)], t_send)
+
+    @pl.when(jnp.logical_not(keeps_one))
+    def _():
+        sent(tin, t_send)
+
+    for step in range(4):
+        z_copy(plane_at(-step), 0, up).wait_send()
+        if step < 3:
+            z_copy(plane_at(step), 1, down).wait_send()
+
+    def k_sent(n, carry):
+        @pl.when(jnp.logical_not(k_to_self(n)))
         def _():
-            for channel in range(2):
-                t_copy(channel, m, me).wait_send()
-
-        return carry
-
-    lax.fori_loop(0, GROUP, t_sent, 0)
+            k_copy(n, k_slot).wait_send()
+
+        return carry
+
+    lax.fori_loop(0, 4, k_sent, 0)
+
     w_own.wait()
 
     def w_wait(n, carry):
@@ -527,7 +528,7 @@
 def block(*operands):
     dma = pltpu.SemaphoreType.DMA
     vmem = pl.BlockSpec(memory_space=pltpu.VMEM)
-    anywhere = pl.BlockSpec(memory_space=pl.ANY)
+    anywhere = pl.BlockSpec(memory_space=pltpu.HBM)
     return pl.pallas_call(
         block_kernel,
         out_shape=(
@@ -576,12 +577,12 @@
             pltpu.VMEM((128, 128), jnp.bfloat16),
             pltpu.VMEM((128, 1024), jnp.bfloat16),
             pltpu.VMEM((512, 128), jnp.bfloat16),
-            dma((9,)),
+            dma((10,)),
             dma((11,)),
             dma((CHUNKS + 1,)),
+            dma,
             dma((GROUP,)),
-            dma((GROUP,)),
-            dma((2, GROUP)),
+            dma,
             dma((2, GROUP)),
             dma((2, NZ)),
             dma((NZ,)),
@@ -593,13 +594,13 @@
             dma((NQ,)),
             dma((NQ,)),
             dma((NQ,)),
-            dma((2, GROUP)),
+            dma,
             dma((2, GROUP)),
             dma((NQ,)),
             dma((NQ,)),
         ],
         compiler_params=pltpu.CompilerParams(
-            collective_id=0, has_side_effects=True, vmem_limit_bytes=60 * 1024 * 1024
+            collective_id=0, has_side_effects=True, vmem_limit_bytes=58 * 1024 * 1024
         ),
         name="pairformer",
     )(*operands)

time: 115 us -> 106 us (0.922)
  Pallas kernels: 111 us -> 102 us
    pallas_call x1, Pallas kernels: 111 us -> 102 us  [block(): pl.pallas_call(block_kernel, out_shape=(jax.ShapeDtypeStruct((1024, 128),...]
where the time goes in v4:
time: 106 us
  Pallas kernels  102 us (96%)
  local copies, waits for them, and re-layouts  2.96 us (3%)
    pallas_call x1, Pallas kernels, block(): pl.pallas_call(block_kernel, out_shape=(jax.ShapeDtypeStruct((1024, 128),...  102 us
    unnamed x2, local copies, waits for them, and re-layouts  2.96 us

profile of v4, /device:TPU:1, one launch (start us, length us, event | category | flops | bytes accessed | tf_op | source)
XLA Modules:
  0.0 105.6 jit_solution(6667893824553096568)
XLA Ops:
  0.6 102.0 %pairformer.1 = (bf16[1024,128]{1,0:T(8,128)(2,1)}, bf16[8,384]{1,0:T(8,128)(2,1)}) custom-call(bf16[8,128,128]{2,1,0:T(8,128)(2,1)} %left_any.1, bf16[64,128,128]{2,1,0:T(8,128)(2,1)} %right_any.1, bf16[1024,128]{1,0:T(8,128)(2,1)} %bitcast.7, bf16[64,384]{1,0:T(8,128)(2,1)} %single_any.1, bf16[128,128]{1,0:T(8,128)(2,1)} %w_gate_any.1, ...), custom_call_target="tpu_custom_call" | custom-call | tf_op jit(solution)/shard_map/pairformer/pallas_call | solution.py:532
  102.6 1.7 %copy.18 = bf16[8,128,128]{2,1,0:T(8,128)(2,1)} copy(bf16[8,128,128]{2,1,0:T(8,128)(2,1)} %bitcast.8) | data formatting | bytes 524288
  104.3 1.3 %copy.19 = bf16[8,384]{1,0:T(8,128)(2,1)} copy(bf16[8,384]{1,0:T(8,128)(2,1)} %get-tuple-element.9) | data formatting | bytes 12288

commit v5 on v4

--- a/solution.py
+++ b/solution.py
@@ -139,9 +139,6 @@
             *group_device(m),
         )
 
-    left_copy.wait()
-    lt[...] = jnp.transpose(left_in[...].astype(jnp.float32), (2, 0, 1)).reshape(GROUP, 16, 128).astype(jnp.bfloat16)
-
     def turn(chunk, carry):
         right_copy(chunk).wait()
         for n in range(1, 16):
@@ -155,20 +152,22 @@
 
     l_own = pltpu.make_async_copy(lt.at[me], l_block(me), own_sem.at[0])
     r_own = pltpu.make_async_copy(rt.at[pl.ds(me * 2, 2)], r_block(me), own_sem.at[4])
+    r_own.start()
+
+    remaining = k_to_self(yh)
+    pl.semaphore_wait(barrier, GROUP + 5 - remaining.astype(jnp.int32))
+    others(lambda m: r_copy(0, m, me).start(), 1, 9)
+    left_copy.wait()
+    lt[...] = jnp.transpose(left_in[...].astype(jnp.float32), (2, 0, 1)).reshape(GROUP, 16, 128).astype(jnp.bfloat16)
     l_own.start()
-    r_own.start()
+    others(lambda m: l_copy(m, me).start())
+    others(lambda m: r_copy(0, m, me).start(), 9, EARLY)
 
     proj_in[...] = jnp.zeros_like(proj_in)
     wo_msg[...] = jnp.zeros_like(wo_msg)
     qg_msg[...] = jnp.zeros_like(qg_msg)
     single_copy.wait()
     single_norm = layer_norm(single[...].astype(jnp.float32), -1).astype(jnp.bfloat16)
-
-    remaining = k_to_self(yh)
-    pl.semaphore_wait(barrier, GROUP + 5 - remaining.astype(jnp.int32))
-    others(lambda m: r_copy(0, m, me).start(), 1, 9)
-    others(lambda m: l_copy(m, me).start())
-    others(lambda m: r_copy(0, m, me).start(), 9, EARLY)
 
     for copy in inputs:
         copy.wait()
@@ -532,8 +531,8 @@
     return pl.pallas_call(
         block_kernel,
         out_shape=(
-            jax.ShapeDtypeStruct((1024, 128), jnp.bfloat16),
-            jax.ShapeDtypeStruct((8, 384), jnp.bfloat16),
+            pltpu.VMEM((1024, 128), jnp.bfloat16),
+            pltpu.VMEM((8, 384), jnp.bfloat16),
         ),
         in_specs=[anywhere] * 14,
         out_specs=(vmem, vmem),

time: 106 us -> 104 us (0.981)
  local copies, waits for them, and re-layouts: 2.96 us -> 1.3 us
    unnamed x2, local copies, waits for them, and re-layouts: 2.96 us -> 1.3 us
where the time goes in v5:
time: 104 us; the launch traced here: 103 us
  Pallas kernels  101 us (97%)
  local copies, waits for them, and re-layouts  1.3 us (1%)
    pallas_call x1, Pallas kernels, block(): pl.pallas_call(block_kernel, out_shape=(pltpu.VMEM((1024, 128), jnp.bfloa...  101 us

profile of v5, /device:TPU:1, one launch (start us, length us, event | category | flops | bytes accessed | tf_op | source)
XLA Modules:
  0.0 103.4 jit_solution(7129688336598850130)
XLA Ops:
  0.6 101.5 %pairformer.1 = (bf16[1024,128]{1,0:T(8,128)(2,1)S(1)}, bf16[8,384]{1,0:T(8,128)(2,1)S(1)}) custom-call(bf16[8,128,128]{2,1,0:T(8,128)(2,1)} %left_any.1, bf16[64,128,128]{2,1,0:T(8,128)(2,1)} %right_any.1, bf16[1024,128]{1,0:T(8,128)(2,1)} %bitcast.8, bf16[64,384]{1,0:T(8,128)(2,1)} %single_any.1, bf16[128,128]{1,0:T(8,128)(2,1)} %w_gate_any.1, ...), custom_call_target="tpu_custom_call" | custom-call | tf_op jit(solution)/shard_map/pairformer/pallas_call | solution.py:531
  102.1 0.7 copy.18
  102.8 0.6 copy.19

commit v6 on v5

--- a/solution.py
+++ b/solution.py
@@ -156,12 +156,12 @@
 
     remaining = k_to_self(yh)
     pl.semaphore_wait(barrier, GROUP + 5 - remaining.astype(jnp.int32))
-    others(lambda m: r_copy(0, m, me).start(), 1, 9)
+    others(lambda m: r_copy(0, m, me).start(), 1, 4)
     left_copy.wait()
     lt[...] = jnp.transpose(left_in[...].astype(jnp.float32), (2, 0, 1)).reshape(GROUP, 16, 128).astype(jnp.bfloat16)
     l_own.start()
     others(lambda m: l_copy(m, me).start())
-    others(lambda m: r_copy(0, m, me).start(), 9, EARLY)
+    others(lambda m: r_copy(0, m, me).start(), 4, EARLY)
 
     proj_in[...] = jnp.zeros_like(proj_in)
     wo_msg[...] = jnp.zeros_like(wo_msg)
@@ -336,22 +336,22 @@
         lax.fori_loop(0, 2, multiply, 0)
         if channel == 0:
             ring_step(kz_copy, 1)
-            q_own.wait()
-
-            def q_wait(n, carry):
-                target = lax.rem(col + n, NQ)
-                q_copy(target, col).wait_send()
-                q_copy(target, target).wait_recv()
-                return carry
-
-            lax.fori_loop(1, NQ, q_wait, 0)
-            for head in range(HEADS):
-                lanes = slice(head * SLOT, head * SLOT + SLOT)
-                q_full[:, lanes] = qg_all[head, :, 0:SLOT]
-                gate_full[:, lanes] = qg_all[head, :, SLOT : 2 * SLOT]
             ring_step(kz_copy, 2)
 
     ring_step(kz_copy, 3)
+    q_own.wait()
+
+    def q_wait(n, carry):
+        target = lax.rem(col + n, NQ)
+        q_copy(target, col).wait_send()
+        q_copy(target, target).wait_recv()
+        return carry
+
+    lax.fori_loop(1, NQ, q_wait, 0)
+    for head in range(HEADS):
+        lanes = slice(head * SLOT, head * SLOT + SLOT)
+        q_full[:, lanes] = qg_all[head, :, 0:SLOT]
+        gate_full[:, lanes] = qg_all[head, :, SLOT : 2 * SLOT]
     ring_end(kz_copy)
 
     low = kv_all[0:HEADS].astype(jnp.float32).reshape(WIDE, 128)

time: 104 us -> 104 us (level)
  no operation moved by 1% of the time
where the time goes in v6:
time: 104 us
  Pallas kernels  102 us (98%)
  local copies, waits for them, and re-layouts  1.3 us (1%)
    pallas_call x1, Pallas kernels, block(): pl.pallas_call(block_kernel, out_shape=(pltpu.VMEM((1024, 128), jnp.bfloa...  102 us

profile of v6, /device:TPU:1, one launch (start us, length us, event | category | flops | bytes accessed | tf_op | source)
XLA Modules:
  0.0 103.7 jit_solution(587492070875819637)
XLA Ops:
  0.6 101.7 %pairformer.1 = (bf16[1024,128]{1,0:T(8,128)(2,1)S(1)}, bf16[8,384]{1,0:T(8,128)(2,1)S(1)}) custom-call(bf16[8,128,128]{2,1,0:T(8,128)(2,1)} %left_any.1, bf16[64,128,128]{2,1,0:T(8,128)(2,1)} %right_any.1, bf16[1024,128]{1,0:T(8,128)(2,1)} %bitcast.8, bf16[64,384]{1,0:T(8,128)(2,1)} %single_any.1, bf16[128,128]{1,0:T(8,128)(2,1)} %w_gate_any.1, ...), custom_call_target="tpu_custom_call" | custom-call | tf_op jit(solution)/shard_map/pairformer/pallas_call | solution.py:531
  102.4 0.7 copy.18
  103.1 0.6 copy.19
